TPU v7x, 256 devices: a whole 4x4x8 slice. The times are simulated.
256 devices in a mesh: span: 4 (over z_hi, core), tok: 64 (over y, z_lo, x).
Axes of the slice: x: 4, y: 4, z: 8 (z_hi: 2, z_lo: 4; z = z_hi * 4 + z_lo), core: 2. Of those that a mesh axis runs over, the one named last changes fastest.
Arguments:
- latent: float32 [4, 2048, 64], P('span', 'tok'), may hold values from -6 to 6
- step_index: int32 [4], replicated, may hold values from 0 to 6
- w_query: bfloat16 [64, 4096], replicated, as said below
- w_key: bfloat16 [64, 4096], replicated, as said below
- w_value: bfloat16 [64, 4096], replicated, may hold values from -0.75 to 0.75
- cond: float32 [3, 4096], replicated, may hold values from -3 to 3
- qk_gain: float32 [2, 32], replicated, may hold values from 0.8 to 6, as said below
- w_out: bfloat16 [4096, 64], replicated, may hold values from -0.09375 to 0.09375
Outputs:
- latent_out: float32 [4, 2048, 64], P('span', 'tok')
- velocity: float32 [4, 2048, 64], P('span', 'tok')
Inputs may be any that keep to these rules, and one draw needn't show every extreme that they name: `w_query`: query projection, fan-in scaled. `w_key`: key projection, fan-in scaled. `qk_gain`: positive gains.
All inputs are finite; a program needn't handle non-finite values.
Results may differ from a plain program's by a relative error of at most 0.008.
Values may be sent and summed in bfloat16 or wider, within the bound.
A program may use at most 64 MiB of HBM per device.

v0:
```python
import functools

import jax
import jax.numpy as jnp
from jax import lax
from jax.experimental import pallas as pl
from jax.experimental.pallas import tpu as pltpu
from jax.sharding import PartitionSpec as P

MESH = pl.DeviceIdType.MESH
NSTEPS = 8
ROWS = 32
CHANS = 64
HEADS = 32
HD = 128
WIDTH = HEADS * HD
SEQ = 2048
PIECE = 4 * ROWS
CHUNK = 16 * ROWS
TILE_HEADS = 8
TILE = TILE_HEADS * ROWS
LOG2E = 1.4426950408889634
BF = jnp.bfloat16
F32 = jnp.float32


def dot_nt(a, b):
    return lax.dot_general(a, b, (((1,), (1,)), ((), ())), preferred_element_type=F32)


def dot_nn(a, b):
    return jnp.dot(a, b, preferred_element_type=F32)


def kernel(
    step_ref, gain_ref, latent_ref, cond_ref, wq_hbm, wk_hbm, wv_hbm, wo_hbm,
    state_out, vel_out,
    grid, wq, wk, wv, wo, aug, state, q2, acc, top, rsc, att,
    wsem, zs, zr, p2s, p2r, p3s, p3r, cs, cr,
):
    c = lax.axis_index("span")
    t = lax.axis_index("tok")
    hi = c // 2
    core = c % 2
    y = t // 16
    zl = (t // 4) % 4
    x = t % 4

    def tok(yy, zz, xx):
        return yy * 16 + zz * 4 + xx

    loads = [
        pltpu.make_async_copy(wk_hbm, wk.at[pl.ds(0, CHANS), :], wsem.at[0]),
        pltpu.make_async_copy(wq_hbm, wq.at[pl.ds(0, CHANS), :], wsem.at[1]),
        pltpu.make_async_copy(wv_hbm, wv.at[pl.ds(0, CHANS), :], wsem.at[2]),
        pltpu.make_async_copy(wo_hbm, wo, wsem.at[3]),
    ]
    for item in loads:
        item.start()

    barrier = pltpu.get_barrier_semaphore()

    def greet(span, token):
        pl.semaphore_signal(barrier, inc=1, device_id=(span, token), device_id_type=MESH)

    other = (1 - hi) * 2 + core
    for d in range(1, 4):
        greet(c, tok(y, (zl + d) % 4, x))
        greet(c, tok((y + d) % 4, zl, x))
        greet(c, tok(y, zl, (x + d) % 4))
    for d in range(4):
        greet(other, tok(y, d, x))
    greet(hi * 2 + 1 - core, t)

    lane = lax.broadcasted_iota(jnp.int32, (1, 128), 1)
    row16 = lax.broadcasted_iota(jnp.int32, (16, WIDTH), 0)
    for which, ref in enumerate((wq, wk, wv)):
        cvec = cond_ref[which : which + 1, :]
        chi = cvec.astype(BF).astype(F32)
        clo = cvec - chi
        rows = jnp.where((row16 == 0) | (row16 == 2), chi, jnp.where(row16 == 1, clo, 0.0))
        ref[CHANS : CHANS + 16, :] = rows.astype(BF)
        ref[CHANS + 16 :, :] = jnp.zeros((128 - CHANS - 16, WIDTH), BF)
    gk = jnp.zeros((1, 128), F32)
    for h in range(HEADS):
        gk = jnp.where((lane == CHANS + h) | (lane == CHANS + HEADS + h), gain_ref[1, h], gk)
    gk = gk * (HD ** (-0.5) * LOG2E)
    selr = lax.broadcasted_iota(jnp.int32, (HEADS, 128), 0)
    sell = lax.broadcasted_iota(jnp.int32, (HEADS, 128), 1)
    sel = jnp.where((sell == CHANS + selr) | (sell == CHANS + HEADS + selr), 1.0, 0.0).astype(BF)
    pmask = jnp.where(lane < CHANS, 1.0, 0.0)
    state[...] = jnp.zeros_like(state)
    state[:, 0:CHANS] = latent_ref[...]

    def sigma(span, extra):
        level = jnp.full((1, 128), step_ref[span] + extra, jnp.int32).astype(F32)
        frac = 1.0 - level / NSTEPS
        return 3.0 * frac / (1.0 + 2.0 * frac)

    pl.semaphore_wait(barrier, 14)
    loads[0].wait()

    def rail(r, kk):
        along_x = kk == r
        return along_x, jnp.where(along_x, x, y), jnp.where(along_x, y, x)

    def inner_tok(along_x, i):
        return jnp.where(along_x, tok(y, zl, i), tok(i, zl, x))

    def outer_tok(along_x, o):
        return jnp.where(along_x, tok(o, zl, x), tok(y, zl, o))

    def rdma(ref, send, recv, dev):
        return pltpu.make_async_remote_copy(
            src_ref=ref, dst_ref=ref, send_sem=send, recv_sem=recv, device_id=dev, device_id_type=MESH
        )

    def step(s, carry):
        for span in range(4):
            sig = sigma(span, s)
            shi = sig.astype(BF).astype(F32)
            slo = sig - shi
            row = jnp.where(
                (lane == CHANS) | (lane == CHANS + 1),
                shi,
                jnp.where(lane == CHANS + 2, slo, jnp.where(lane == CHANS + 3, 1.0, 0.0)),
            )
            aug[span] = jnp.broadcast_to(row, (8, 128))
        patches = state[...]
        own = (patches + aug[c][0:1, :]).astype(BF)

        squares = jnp.zeros((ROWS, 128), F32)
        for h in range(HEADS):
            pk = dot_nn(own, wk[:, h * HD : (h + 1) * HD])
            ms = jnp.sum(pk * pk, axis=-1, keepdims=True)
            squares = jnp.where((lane == CHANS + h) | (lane == CHANS + HEADS + h), ms, squares)
        factor = gk / jnp.sqrt(squares * (1.0 / HD) + 1e-06)
        fhi = factor.astype(BF).astype(F32)
        row = jnp.where(lane < CHANS, patches, jnp.where(lane < CHANS + HEADS, fhi, factor - fhi))
        _, inner0, outer0 = rail(hi, core)
        first = (outer0 * 16 + inner0 * 4 + zl) * ROWS
        grid[s, c, pl.ds(pl.multiple_of(first, ROWS), ROWS), :] = row.astype(BF)

        def zblock(e, zz):
            r = e // 2
            _, i, o = rail(r, e % 2)
            at = pl.multiple_of((o * 16 + i * 4 + zz) * ROWS, ROWS)
            return grid.at[s, e, pl.ds(at, ROWS), :]

        def piece(e, o, i):
            at = pl.multiple_of((o * 4 + i) * PIECE, PIECE)
            return grid.at[s, e, pl.ds(at, PIECE), :]

        def chunk_of(e, o):
            at = pl.multiple_of(o * CHUNK, CHUNK)
            return grid.at[s, e, pl.ds(at, CHUNK), :]

        def z_copy(d):
            return rdma(zblock(c, zl), zs.at[s, d - 1], zr.at[s, hi, zl], (c, tok(y, (zl + d) % 4, x)))

        def up_copy(d):
            return rdma(zblock(c, zl), zs.at[s, 3 + d], zr.at[s, 0, zl], (other, tok(y, d, x)))

        def z_wait(r, zz):
            e = core + 2 * r
            rdma(zblock(e, zz), zs.at[s, 0], zr.at[s, r, zz], (c, t)).wait_recv()

        for d in range(1, 4):
            z_copy(d).start()

        @pl.when(hi == 0)
        def _():
            for d in range(4):
                up_copy(d).start()

        def p2_copy(r, d):
            e = core + 2 * r
            along_x, i, o = rail(r, core)
            return rdma(piece(e, o, i), p2s.at[s, r, d - 1], p2r.at[s, r, i], (c, inner_tok(along_x, (i + d) % 4)))

        def p3_copy(r, i, d):
            e = core + 2 * r
            along_x, _, o = rail(r, core)
            return rdma(
                piece(e, o, i), p3s.at[s, r, i, d - 1], p3r.at[s, r, o, i], (c, outer_tok(along_x, (o + d) % 4))
            )

        def core_copy(r, o):
            e = core + 2 * r
            return rdma(chunk_of(e, o), cs.at[s, r, o], cr.at[s, r, o], (hi * 2 + 1 - core, t))

        @pl.when(s == 0)
        def _():
            loads[1].wait()

        for h in range(HEADS):
            pq = dot_nn(own, wq[:, h * HD : (h + 1) * HD])
            ms = jnp.sum(pq * pq, axis=-1, keepdims=True) * (1.0 / HD)
            qn = (pq / jnp.sqrt(ms + 1e-06) * gain_ref[0, h]).astype(BF)
            qk = dot_nt(qn, wk[:, h * HD : (h + 1) * HD])
            qhi = qk.astype(BF)
            q2[h * ROWS : (h + 1) * ROWS, 0:128] = qhi
            q2[h * ROWS : (h + 1) * ROWS, 128:256] = (qk - qhi.astype(F32)).astype(BF)
        acc[...] = jnp.zeros_like(acc)
        top[...] = jnp.full_like(top, -1e30)

        def second(r, carry):
            @pl.when(r == hi)
            def _():
                for d in range(1, 4):
                    z_wait(r, (zl + d) % 4)

            @pl.when(r != hi)
            def _():
                for d in range(4):
                    z_wait(r, d)

            _, i, _ = rail(r, core)
            for d in range(1, 4):
                p2_copy(r, d).start()
            for d in range(1, 4):
                p3_copy(r, i, d).start()
            return carry

        lax.fori_loop(0, hi + 1, second, 0)

        def third(r, carry):
            e = core + 2 * r
            _, i, o = rail(r, core)
            for d in range(1, 4):
                ii = (i + d) % 4
                rdma(piece(e, o, ii), p2s.at[s, r, 0], p2r.at[s, r, ii], (c, t)).wait_recv()
                for dd in range(1, 4):
                    p3_copy(r, ii, dd).start()
            return carry

        lax.fori_loop(0, hi + 1, third, 0)

        def attend(e, o):
            g = chunk_of(e, o)[...]
            g2 = (g * pmask.astype(BF) + aug[e][0:1, :].astype(BF))
            keys = jnp.concatenate([g2, g2], axis=1)
            rsc[...] = dot_nt(sel, g)
            for tile in range(HEADS // TILE_HEADS):
                base = tile * TILE
                scores = dot_nt(q2[base : base + TILE, :], keys)
                parts = []
                for k in range(TILE_HEADS):
                    h = tile * TILE_HEADS + k
                    at = slice(h * ROWS, (h + 1) * ROWS)
                    sh = scores[k * ROWS : (k + 1) * ROWS, :] * rsc[h : h + 1, :]
                    old = top[at, :]
                    new = jnp.maximum(old, jnp.max(sh, axis=-1, keepdims=True))
                    top[at, :] = new
                    acc[at, :] = acc[at, :] * jnp.exp2(old - new)
                    parts.append(jnp.exp2(sh - new[:, 0:1]).astype(BF))
                acc[base : base + TILE, :] += dot_nn(jnp.concatenate(parts, axis=0), g2)

        def outer_loop(k, carry):
            off = k ^ (k // 2)

            def inner_loop(j, carry):
                mine = j <= hi
                e = jnp.where(mine, c - 2 * j, c - 1 - 2 * (j - hi - 1))
                r = e // 2
                _, _, o = rail(r, e % 2)
                b = (o + off) % 4

                @pl.when(mine)
                def _():
                    @pl.when(k > 0)
                    def _():
                        for i in range(4):
                            rdma(piece(e, b, i), p3s.at[s, r, 0, 0], p3r.at[s, r, b, i], (c, t)).wait_recv()

                    @pl.when(r <= hi - core)
                    def _():
                        core_copy(r, b).start()

                @pl.when(jnp.logical_not(mine))
                def _():
                    rdma(chunk_of(e, b), cs.at[s, 0, 0], cr.at[s, r, b], (c, t)).wait_recv()

                attend(e, b)
                return carry

            lax.fori_loop(0, c + 1, inner_loop, 0)
            return carry

        lax.fori_loop(0, 4, outer_loop, 0)

        @pl.when(s == 0)
        def _():
            loads[2].wait()
            loads[3].wait()

        for h in range(HEADS):
            a = acc[h * ROWS : (h + 1) * ROWS, :]
            z = a / a[:, CHANS + 3 : CHANS + 4]
            zhi = z.astype(BF)
            zlo = (z - zhi.astype(F32)).astype(BF)
            both = dot_nn(jnp.concatenate([zhi, zlo], axis=0), wv[:, h * HD : (h + 1) * HD])
            att[:, h * HD : (h + 1) * HD] = (both[0:ROWS] + both[ROWS:]).astype(BF)
        velocity = dot_nn(att[...], wo[...])
        change = sigma(c, s + 1) - sigma(c, s)
        state[:, 0:CHANS] = state[:, 0:CHANS] + change[:, 0:CHANS] * velocity
        vel_out[...] = velocity

        for d in range(1, 4):
            z_copy(d).wait_send()

        @pl.when(hi == 0)
        def _():
            for d in range(4):
                up_copy(d).wait_send()

        def drain(r, carry):
            for d in range(1, 4):
                p2_copy(r, d).wait_send()
            for i in range(4):
                for d in range(1, 4):
                    p3_copy(r, i, d).wait_send()

            @pl.when(r <= hi - core)
            def _():
                for o in range(4):
                    core_copy(r, o).wait_send()

            return carry

        lax.fori_loop(0, hi + 1, drain, 0)
        return carry

    lax.fori_loop(0, 2, step, 0)
    state_out[...] = state[:, 0:CHANS]


def local(latent, step_index, w_query, w_key, w_value, cond, qk_gain, w_out):
    vmem = pl.BlockSpec(memory_space=pltpu.VMEM)
    smem = pl.BlockSpec(memory_space=pltpu.SMEM)
    hbm = pl.BlockSpec(memory_space=pl.ANY)
    dma = pltpu.SemaphoreType.DMA
    out = jax.ShapeDtypeStruct((ROWS, CHANS), F32)
    state, velocity = pl.pallas_call(
        kernel,
        out_shape=(out, out),
        in_specs=[smem, smem, vmem, vmem, hbm, hbm, hbm, hbm],
        out_specs=(vmem, vmem),
        scratch_shapes=[
            pltpu.VMEM((2, 4, SEQ, 128), BF),
            pltpu.VMEM((128, WIDTH), BF),
            pltpu.VMEM((128, WIDTH), BF),
            pltpu.VMEM((128, WIDTH), BF),
            pltpu.VMEM((WIDTH, CHANS), BF),
            pltpu.VMEM((4, 8, 128), F32),
            pltpu.VMEM((ROWS, 128), F32),
            pltpu.VMEM((HEADS * ROWS, 256), BF),
            pltpu.VMEM((HEADS * ROWS, 128), F32),
            pltpu.VMEM((HEADS * ROWS, 128), F32),
            pltpu.VMEM((HEADS, CHUNK), F32),
            pltpu.VMEM((ROWS, WIDTH), BF),
            dma((4,)),
            dma((2, 7)),
            dma((2, 2, 4)),
            dma((2, 2, 3)),
            dma((2, 2, 4)),
            dma((2, 2, 4, 3)),
            dma((2, 2, 4, 4)),
            dma((2, 2, 4)),
            dma((2, 2, 4)),
        ],
        compiler_params=pltpu.CompilerParams(
            collective_id=0, has_side_effects=True, vmem_limit_bytes=48 * 1024 * 1024
        ),
    )(step_index, qk_gain, latent[0], cond, w_query, w_key, w_value, w_out)
    return state[None], velocity[None]


def solution(mesh):
    return jax.shard_map(
        local,
        mesh=mesh,
        in_specs=(P("span", "tok", None), P(), P(), P(), P(), P(), P(), P()),
        out_specs=(P("span", "tok", None), P("span", "tok", None)),
        check_vma=False,
    )
```

profile of v0, /device:TPU:225, one launch (start us, length us, event | category | flops | bytes accessed | tf_op | source)
XLA Modules:
  0.0 95.5 jit_solution(14057441248020674122)
XLA Ops:
  0.6 0.0 copy-start
  0.6 0.0 copy-start.1
  0.7 0.0 copy-start.2
  0.7 1.6 %copy.10.wo_hbm = bf16[4096,64]{1,0:T(8,128)(2,1)S(1)} copy(bf16[4096,64]{0,1:T(8,128)(2,1)} %param.15) | data formatting | bytes 1048576 | tf_op args[7]
  2.3 0.0 copy-done
  2.3 0.0 copy-done.1
  2.3 0.0 copy-done.2
  2.3 0.0 copy-start.3
  2.3 0.8 copy-done.3
  3.2 0.0 copy-start.4
  3.2 0.7 copy-done.4
  3.9 0.0 copy-start.5
  3.9 0.7 copy-done.5
  4.6 0.0 copy-start.6
  4.6 0.7 copy-done.6
  5.2 89.1 %shard_map.95 = (f32[32,64]{1,0:T(8,128)S(1)}, f32[32,64]{1,0:T(8,128)S(1)}) custom-call(s32[4]{0:T(128)S(1)} %copy-done.6, f32[2,32]{1,0:T(2,128)S(1)} %copy-done.5, f32[32,64]{1,0:T(8,128)S(1)} %bitcast.3, f32[3,4096]{1,0:T(4,128)S(1)} %copy-done.3, bf16[64,4096]{1,0:T(8,128)(2,1)S(1)} %copy-done, bf16[64,4096]{1,0:T(8,128)(2,1)S(1)} %copy-done.1, ...), custom_call_target="tpu_custom_call" | custom-call | tf_op jit(solution)/shard_map/pallas_call | solution.py:344
  94.3 0.6 copy.13
  94.9 0.6 copy.14
Async XLA Ops:
  0.6 1.7 %copy-start = (bf16[64,4096]{1,0:T(8,128)(2,1)S(1)}, bf16[64,4096]{1,0:T(8,128)(2,1)}, u32[]{:S(2)}) copy-start(bf16[64,4096]{1,0:T(8,128)(2,1)} %wq_hbm.1) | copy-start | bytes 1572868
  0.6 1.7 %copy-start.1 = (bf16[64,4096]{1,0:T(8,128)(2,1)S(1)}, bf16[64,4096]{1,0:T(8,128)(2,1)}, u32[]{:S(2)}) copy-start(bf16[64,4096]{1,0:T(8,128)(2,1)} %wk_hbm.1) | copy-start | bytes 1572868
  0.7 1.7 %copy-start.2 = (bf16[64,4096]{1,0:T(8,128)(2,1)S(1)}, bf16[64,4096]{1,0:T(8,128)(2,1)}, u32[]{:S(2)}) copy-start(bf16[64,4096]{1,0:T(8,128)(2,1)} %wv_hbm.1) | copy-start | bytes 1572868
  2.3 0.8 copy-start.3
  3.2 0.7 copy-start.4
  3.9 0.7 copy-start.5
  4.6 0.7 copy-start.6
where the time goes:
time: 95.8 us; the launch traced here: 95.5 us
  Pallas kernels  89.1 us (93%)
  local copies, waits for them, and re-layouts  5.74 us (6%)
    pallas_call x1, Pallas kernels, local(): pl.pallas_call(kernel, out_shape=(out, out), in_specs=[smem, smem, vmem,...  89.1 us
    unnamed x17, local copies, waits for them, and re-layouts  5.74 us

commit v1 on v0

--- a/solution.py
+++ b/solution.py
@@ -17,8 +17,10 @@
 SEQ = 2048
 PIECE = 4 * ROWS
 CHUNK = 16 * ROWS
-TILE_HEADS = 8
-TILE = TILE_HEADS * ROWS
+QUERIES = HEADS * ROWS
+COLS = QUERIES // 2
+GROUP = 4
+SUB = 64
 LOG2E = 1.4426950408889634
 BF = jnp.bfloat16
 F32 = jnp.float32
@@ -35,7 +37,7 @@
 def kernel(
     step_ref, gain_ref, latent_ref, cond_ref, wq_hbm, wk_hbm, wv_hbm, wo_hbm,
     state_out, vel_out,
-    grid, wq, wk, wv, wo, aug, state, q2, acc, top, rsc, att,
+    grid, wq, wk, wv, wo, aug, state, q2, flat, acc, top,
     wsem, zs, zr, p2s, p2r, p3s, p3r, cs, cr,
 ):
     c = lax.axis_index("span")
@@ -85,9 +87,10 @@
     for h in range(HEADS):
         gk = jnp.where((lane == CHANS + h) | (lane == CHANS + HEADS + h), gain_ref[1, h], gk)
     gk = gk * (HD ** (-0.5) * LOG2E)
-    selr = lax.broadcasted_iota(jnp.int32, (HEADS, 128), 0)
-    sell = lax.broadcasted_iota(jnp.int32, (HEADS, 128), 1)
-    sel = jnp.where((sell == CHANS + selr) | (sell == CHANS + HEADS + selr), 1.0, 0.0).astype(BF)
+    down = lax.broadcasted_iota(jnp.int32, (128, 128), 0)
+    across = lax.broadcasted_iota(jnp.int32, (128, 128), 1)
+    spread = jnp.where((down >= CHANS) & (down % HEADS == across % HEADS), 1.0, 0.0).astype(BF)
+    eye = jnp.where(down == across, 1.0, 0.0).astype(BF)
     pmask = jnp.where(lane < CHANS, 1.0, 0.0)
     state[...] = jnp.zeros_like(state)
     state[:, 0:CHANS] = latent_ref[...]
@@ -130,9 +133,10 @@
         own = (patches + aug[c][0:1, :]).astype(BF)
 
         squares = jnp.zeros((ROWS, 128), F32)
+        pk = dot_nn(own, wk[...])
         for h in range(HEADS):
-            pk = dot_nn(own, wk[:, h * HD : (h + 1) * HD])
-            ms = jnp.sum(pk * pk, axis=-1, keepdims=True)
+            part = pk[:, h * HD : (h + 1) * HD]
+            ms = jnp.sum(part * part, axis=-1, keepdims=True)
             squares = jnp.where((lane == CHANS + h) | (lane == CHANS + HEADS + h), ms, squares)
         factor = gk / jnp.sqrt(squares * (1.0 / HD) + 1e-06)
         fhi = factor.astype(BF).astype(F32)
@@ -193,14 +197,18 @@
         def _():
             loads[1].wait()
 
+        pq = dot_nn(own, wq[...])
+        normed = []
         for h in range(HEADS):
-            pq = dot_nn(own, wq[:, h * HD : (h + 1) * HD])
-            ms = jnp.sum(pq * pq, axis=-1, keepdims=True) * (1.0 / HD)
-            qn = (pq / jnp.sqrt(ms + 1e-06) * gain_ref[0, h]).astype(BF)
-            qk = dot_nt(qn, wk[:, h * HD : (h + 1) * HD])
-            qhi = qk.astype(BF)
-            q2[h * ROWS : (h + 1) * ROWS, 0:128] = qhi
-            q2[h * ROWS : (h + 1) * ROWS, 128:256] = (qk - qhi.astype(F32)).astype(BF)
+            part = pq[:, h * HD : (h + 1) * HD]
+            ms = jnp.sum(part * part, axis=-1, keepdims=True) * (1.0 / HD)
+            normed.append((part / jnp.sqrt(ms + 1e-06) * gain_ref[0, h]).astype(BF))
+        for h in range(HEADS):
+            flat[pl.ds(h, ROWS, stride=HEADS), :] = dot_nt(normed[h], wk[:, h * HD : (h + 1) * HD])
+        qk = flat[...]
+        qhi = qk.astype(BF)
+        q2[:, 0:128] = qhi
+        q2[:, 128:256] = (qk - qhi.astype(F32)).astype(BF)
         acc[...] = jnp.zeros_like(acc)
         top[...] = jnp.full_like(top, -1e30)
 
@@ -236,35 +244,61 @@
 
         lax.fori_loop(0, hi + 1, third, 0)
 
-        def attend(e, o):
-            g = chunk_of(e, o)[...]
-            g2 = (g * pmask.astype(BF) + aug[e][0:1, :].astype(BF))
-            keys = jnp.concatenate([g2, g2], axis=1)
-            rsc[...] = dot_nt(sel, g)
-            for tile in range(HEADS // TILE_HEADS):
-                base = tile * TILE
-                scores = dot_nt(q2[base : base + TILE, :], keys)
-                parts = []
-                for k in range(TILE_HEADS):
-                    h = tile * TILE_HEADS + k
-                    at = slice(h * ROWS, (h + 1) * ROWS)
-                    sh = scores[k * ROWS : (k + 1) * ROWS, :] * rsc[h : h + 1, :]
-                    old = top[at, :]
-                    new = jnp.maximum(old, jnp.max(sh, axis=-1, keepdims=True))
-                    top[at, :] = new
-                    acc[at, :] = acc[at, :] * jnp.exp2(old - new)
-                    parts.append(jnp.exp2(sh - new[:, 0:1]).astype(BF))
-                acc[base : base + TILE, :] += dot_nn(jnp.concatenate(parts, axis=0), g2)
-
-        def outer_loop(k, carry):
-            off = k ^ (k // 2)
-
-            def inner_loop(j, carry):
-                mine = j <= hi
-                e = jnp.where(mine, c - 2 * j, c - 1 - 2 * (j - hi - 1))
-                r = e // 2
-                _, _, o = rail(r, e % 2)
-                b = (o + off) % 4
+        def attend(blocks):
+            keys, factors, turned = [], [], []
+            for e, o in blocks:
+                g = chunk_of(e, o)[...]
+                g2 = g * pmask.astype(BF) + aug[e][0:1, :].astype(BF)
+                keys.append(jnp.concatenate([g2, g2], axis=1))
+                factors.append(dot_nn(g, spread))
+                turned.append(dot_nt(eye, g2).astype(BF))
+            units = [(k, u) for k in range(len(blocks)) for u in range(QUERIES // COLS)]
+
+            def score(n):
+                k, u = units[n]
+                return dot_nt(keys[k], q2[u * COLS : (u + 1) * COLS, :])
+
+            def soften(n, raw):
+                k, u = units[n]
+                cols = slice(u * COLS, (u + 1) * COLS)
+                scaled, best = [], None
+                for at in range(0, CHUNK, SUB):
+                    wide = jnp.concatenate([factors[k][at : at + SUB, :]] * (COLS // 128), axis=1)
+                    part = raw[at : at + SUB, :] * wide
+                    scaled.append(part)
+                    high = jnp.max(part.reshape(SUB // 8, 8, COLS), axis=0)
+                    best = high if best is None else jnp.maximum(best, high)
+                old = top[0:1, cols]
+                new = jnp.maximum(old, jnp.max(best, axis=0, keepdims=True))
+                top[0:1, cols] = new
+                weights = [jnp.exp2(part - new).astype(BF) for part in scaled]
+                return n, jnp.concatenate(weights, axis=0), jnp.exp2(old - new)
+
+            def gather(n, weights, alpha):
+                k, u = units[n]
+                cols = slice(u * COLS, (u + 1) * COLS)
+                acc[:, cols] = acc[:, cols] * alpha + dot_nn(turned[k], weights)
+
+            raw = score(0)
+            pending = None
+            for n in range(len(units)):
+                later = score(n + 1) if n + 1 < len(units) else None
+                ready = soften(n, raw)
+                if pending is not None:
+                    gather(*pending)
+                pending, raw = ready, later
+            gather(*pending)
+
+        def place(n):
+            k, j = n // (c + 1), n % (c + 1)
+            mine = j <= hi
+            e = jnp.where(mine, c - 2 * j, c - 1 - 2 * (j - hi - 1))
+            _, _, o = rail(e // 2, e % 2)
+            return k, mine, e, e // 2, (o + (k ^ (k // 2))) % 4
+
+        def group(m, carry):
+            def arrive(q, carry):
+                k, mine, e, r, b = place(GROUP * m + q)
 
                 @pl.when(mine)
                 def _():
@@ -277,31 +311,43 @@
                     def _():
                         core_copy(r, b).start()
 
+                return carry
+
+            def cross(q, carry):
+                k, mine, e, r, b = place(GROUP * m + q)
+
                 @pl.when(jnp.logical_not(mine))
                 def _():
                     rdma(chunk_of(e, b), cs.at[s, 0, 0], cr.at[s, r, b], (c, t)).wait_recv()
 
-                attend(e, b)
                 return carry
 
-            lax.fori_loop(0, c + 1, inner_loop, 0)
+            lax.fori_loop(0, GROUP, arrive, 0)
+            lax.fori_loop(0, GROUP, cross, 0)
+            blocks = []
+            for q in range(GROUP):
+                _, _, e, _, b = place(GROUP * m + q)
+                blocks.append((e, b))
+            attend(blocks)
             return carry
 
-        lax.fori_loop(0, 4, outer_loop, 0)
+        lax.fori_loop(0, c + 1, group, 0)
 
         @pl.when(s == 0)
         def _():
             loads[2].wait()
             loads[3].wait()
 
+        sums = acc[...]
+        flat[...] = (sums / sums[CHANS + 3 : CHANS + 4, :]).T
+        attended = []
         for h in range(HEADS):
-            a = acc[h * ROWS : (h + 1) * ROWS, :]
-            z = a / a[:, CHANS + 3 : CHANS + 4]
+            z = flat[pl.ds(h, ROWS, stride=HEADS), :]
             zhi = z.astype(BF)
             zlo = (z - zhi.astype(F32)).astype(BF)
             both = dot_nn(jnp.concatenate([zhi, zlo], axis=0), wv[:, h * HD : (h + 1) * HD])
-            att[:, h * HD : (h + 1) * HD] = (both[0:ROWS] + both[ROWS:]).astype(BF)
-        velocity = dot_nn(att[...], wo[...])
+            attended.append((both[0:ROWS] + both[ROWS:]).astype(BF))
+        velocity = dot_nt(jnp.concatenate(attended, axis=1), wo[...])
         change = sigma(c, s + 1) - sigma(c, s)
         state[:, 0:CHANS] = state[:, 0:CHANS] + change[:, 0:CHANS] * velocity
         vel_out[...] = velocity
@@ -351,14 +397,13 @@
             pltpu.VMEM((128, WIDTH), BF),
             pltpu.VMEM((128, WIDTH), BF),
             pltpu.VMEM((128, WIDTH), BF),
-            pltpu.VMEM((WIDTH, CHANS), BF),
+            pltpu.VMEM((CHANS, WIDTH), BF),
             pltpu.VMEM((4, 8, 128), F32),
             pltpu.VMEM((ROWS, 128), F32),
-            pltpu.VMEM((HEADS * ROWS, 256), BF),
-            pltpu.VMEM((HEADS * ROWS, 128), F32),
-            pltpu.VMEM((HEADS * ROWS, 128), F32),
-            pltpu.VMEM((HEADS, CHUNK), F32),
-            pltpu.VMEM((ROWS, WIDTH), BF),
+            pltpu.VMEM((QUERIES, 256), BF),
+            pltpu.VMEM((QUERIES, 128), F32),
+            pltpu.VMEM((128, QUERIES), F32),
+            pltpu.VMEM((8, QUERIES), F32),
             dma((4,)),
             dma((2, 7)),
             dma((2, 2, 4)),
@@ -372,7 +417,7 @@
         compiler_params=pltpu.CompilerParams(
             collective_id=0, has_side_effects=True, vmem_limit_bytes=48 * 1024 * 1024
         ),
-    )(step_index, qk_gain, latent[0], cond, w_query, w_key, w_value, w_out)
+    )(step_index, qk_gain, latent[0], cond, w_query, w_key, w_value, w_out.T)
     return state[None], velocity[None]
 
 

time: 95.8 us -> 75.6 us (0.79)
  the two profiles are of different devices: /device:TPU:225 before, /device:TPU:226 now
where the time goes in v1:
time: 75.6 us; the launch traced here: 75.2 us
  Pallas kernels  67 us (89%)
  local copies, waits for them, and re-layouts  7.6 us (10%)
    pallas_call x1, Pallas kernels, local(): pl.pallas_call(kernel, out_shape=(out, out), in_specs=[smem, smem, vmem,...  67 us
    unnamed x18, local copies, waits for them, and re-layouts  7.6 us

profile of v1, /device:TPU:226, one launch (start us, length us, event | category | flops | bytes accessed | tf_op | source)
XLA Modules:
  0.0 75.2 jit_solution(11876587299179383140)
XLA Ops:
  0.6 0.0 copy-start.6
  0.6 0.0 copy-start.7
  0.7 0.7 copy-done.6
  1.3 0.0 copy-done.7
  1.3 0.0 copy-start
  1.3 1.0 %copy-done = bf16[64,4096]{1,0:T(8,128)(2,1)S(1)} copy-done((bf16[64,4096]{1,0:T(8,128)(2,1)S(1)}, bf16[64,4096]{1,0:T(8,128)(2,1)}, u32[]{:S(2)}) %copy-start) | copy-done | bytes 524312
  2.4 0.0 copy-start.1
  2.4 1.0 %copy-done.1 = bf16[64,4096]{1,0:T(8,128)(2,1)S(1)} copy-done((bf16[64,4096]{1,0:T(8,128)(2,1)S(1)}, bf16[64,4096]{1,0:T(8,128)(2,1)}, u32[]{:S(2)}) %copy-start.1) | copy-done | bytes 524312
  3.4 0.0 copy-start.2
  3.4 1.0 %copy-done.2 = bf16[64,4096]{1,0:T(8,128)(2,1)S(1)} copy-done((bf16[64,4096]{1,0:T(8,128)(2,1)S(1)}, bf16[64,4096]{1,0:T(8,128)(2,1)}, u32[]{:S(2)}) %copy-start.2) | copy-done | bytes 524312
  4.4 0.0 copy-start.3
  4.4 1.0 %copy-done.3 = bf16[4096,64]{0,1:T(8,128)(2,1)S(1)} copy-done((bf16[4096,64]{0,1:T(8,128)(2,1)S(1)}, bf16[4096,64]{0,1:T(8,128)(2,1)}, u32[]{:S(2)}) %copy-start.3) | copy-done | bytes 524312
  5.5 0.0 copy-start.4
  5.5 0.8 %copy-done.4 = f32[3,4096]{1,0:T(4,128)S(1)} copy-done((f32[3,4096]{1,0:T(4,128)S(1)}, f32[3,4096]{1,0:T(4,128)}, u32[]{:S(2)}) %copy-start.4) | copy-done | bytes 49176
  6.3 0.0 copy-start.5
  6.3 0.7 copy-done.5
  7.0 67.0 %shard_map.95 = (f32[32,64]{1,0:T(8,128)S(1)}, f32[32,64]{1,0:T(8,128)S(1)}) custom-call(s32[4]{0:T(128)S(1)} %copy-done.7, f32[2,32]{1,0:T(2,128)S(1)} %copy-done.6, f32[32,64]{1,0:T(8,128)S(1)} %bitcast.5, f32[3,4096]{1,0:T(4,128)S(1)} %copy-done.4, bf16[64,4096]{1,0:T(8,128)(2,1)S(1)} %copy-done, bf16[64,4096]{1,0:T(8,128)(2,1)S(1)} %copy-done.1, ...), custom_call_target="tpu_custom_call" | custom-call | tf_op jit(solution)/shard_map/pallas_call | solution.py:390
  74.0 0.6 copy.12
  74.6 0.6 copy.13
Async XLA Ops:
  0.6 0.7 copy-start.6
  0.6 0.7 copy-start.7
  1.3 1.0 %copy-start = (bf16[64,4096]{1,0:T(8,128)(2,1)S(1)}, bf16[64,4096]{1,0:T(8,128)(2,1)}, u32[]{:S(2)}) copy-start(bf16[64,4096]{1,0:T(8,128)(2,1)} %wq_hbm.1) | copy-start | bytes 1572868
  2.4 1.0 %copy-start.1 = (bf16[64,4096]{1,0:T(8,128)(2,1)S(1)}, bf16[64,4096]{1,0:T(8,128)(2,1)}, u32[]{:S(2)}) copy-start(bf16[64,4096]{1,0:T(8,128)(2,1)} %wk_hbm.1) | copy-start | bytes 1572868
  3.4 1.0 %copy-start.2 = (bf16[64,4096]{1,0:T(8,128)(2,1)S(1)}, bf16[64,4096]{1,0:T(8,128)(2,1)}, u32[]{:S(2)}) copy-start(bf16[64,4096]{1,0:T(8,128)(2,1)} %wv_hbm.1) | copy-start | bytes 1572868
  4.4 1.0 %copy-start.3 = (bf16[4096,64]{0,1:T(8,128)(2,1)S(1)}, bf16[4096,64]{0,1:T(8,128)(2,1)}, u32[]{:S(2)}) copy-start(bf16[4096,64]{0,1:T(8,128)(2,1)} %param.15) | copy-start | bytes 1572868
  5.5 0.8 %copy-start.4 = (f32[3,4096]{1,0:T(4,128)S(1)}, f32[3,4096]{1,0:T(4,128)}, u32[]{:S(2)}) copy-start(f32[3,4096]{1,0:T(4,128)} %cond_ref.1) | copy-start | bytes 147460
  6.3 0.7 copy-start.5

commit v2 on v1

v2 whole, which is shorter than its diff:
```python
import jax
import jax.numpy as jnp
from jax import lax
from jax.experimental import pallas as pl
from jax.experimental.pallas import tpu as pltpu
from jax.sharding import PartitionSpec as P

MESH = pl.DeviceIdType.MESH
NSTEPS = 8
ROWS = 32
HALF = 16
CHANS = 64
HEADS = 32
HD = 128
WIDTH = HEADS * HD
SEQ = 2048
CHUNK = SEQ // 4
QUERIES = HEADS * ROWS
COLS = QUERIES // 2
SUB = 64
LAG = 2
LOG2E = 1.4426950408889634
BF = jnp.bfloat16
F32 = jnp.float32


def dot_nt(a, b):
    return lax.dot_general(a, b, (((1,), (1,)), ((), ())), preferred_element_type=F32)


def dot_nn(a, b):
    return jnp.dot(a, b, preferred_element_type=F32)


def kernel(
    step_ref, gain_ref, latent_ref, cond_ref, wq_hbm, wk_hbm, wv_hbm, wo_hbm,
    state_out, vel_out,
    grid, wq, wk, wv, wo, aug, state, swap, result, back, q2, flat, acc, top, accx, topx,
    wsem, zs, zr, p2s, p2r, p3s, p3r, cs, cr, xs, xr,
):
    c = lax.axis_index("span")
    t = lax.axis_index("tok")
    zhi = c // 2
    core = c % 2
    kind = jnp.where(zhi == core, 0, 1)
    y = t // 16
    zl = (t // 4) % 4
    x = t % 4
    z = zhi * 4 + zl
    along_x = kind == 0
    inner = jnp.where(along_x, x, y)
    outer = jnp.where(along_x, y, x)

    def tok(yy, zz, xx):
        return yy * 16 + zz * 4 + xx

    def z_peer(d):
        zz = (z + d) % 8
        up = zz // 4
        return kind + up * (3 - 2 * kind), tok(y, zz % 4, x)

    def inner_peer(d):
        i = (inner + d) % 4
        return c, jnp.where(along_x, tok(y, zl, i), tok(i, zl, x))

    def outer_peer(d):
        o = (outer + d) % 4
        return c, jnp.where(along_x, tok(o, zl, x), tok(y, zl, o))

    mate = (zhi * 2 + 1 - core, t)

    loads = [
        pltpu.make_async_copy(wk_hbm, wk.at[pl.ds(0, CHANS), :], wsem.at[0]),
        pltpu.make_async_copy(wq_hbm, wq.at[pl.ds(0, CHANS), :], wsem.at[1]),
        pltpu.make_async_copy(wv_hbm, wv.at[pl.ds(0, CHANS), :], wsem.at[2]),
        pltpu.make_async_copy(wo_hbm, wo, wsem.at[3]),
    ]
    for item in loads:
        item.start()

    barrier = pltpu.get_barrier_semaphore()

    def greet(dev):
        pl.semaphore_signal(barrier, inc=1, device_id=dev, device_id_type=MESH)

    for d in range(1, 8):
        greet(z_peer(d))
    for d in range(1, 4):
        greet(inner_peer(d))
        greet(outer_peer(d))
    greet(mate)

    lane = lax.broadcasted_iota(jnp.int32, (1, 128), 1)
    low = lax.broadcasted_iota(jnp.int32, (ROWS, 128), 0) < HALF
    row16 = lax.broadcasted_iota(jnp.int32, (16, WIDTH), 0)
    for which, ref in enumerate((wq, wk, wv)):
        cvec = cond_ref[which : which + 1, :]
        chi = cvec.astype(BF).astype(F32)
        clo = cvec - chi
        rows = jnp.where((row16 == 0) | (row16 == 2), chi, jnp.where(row16 == 1, clo, 0.0))
        ref[CHANS : CHANS + 16, :] = rows.astype(BF)
        ref[CHANS + 16 :, :] = jnp.zeros((128 - CHANS - 16, WIDTH), BF)
    gk = jnp.zeros((1, 128), F32)
    for h in range(HEADS):
        gk = jnp.where((lane == CHANS + h) | (lane == CHANS + HEADS + h), gain_ref[1, h], gk)
    gk = gk * (HD ** (-0.5) * LOG2E)
    down = lax.broadcasted_iota(jnp.int32, (128, 128), 0)
    across = lax.broadcasted_iota(jnp.int32, (128, 128), 1)
    spread = jnp.where((down >= CHANS) & (down % HEADS == across % HEADS), 1.0, 0.0).astype(BF)
    eye = jnp.where(down == across, 1.0, 0.0).astype(BF)
    pmask = jnp.where(lane < CHANS, 1.0, 0.0)
    state[...] = jnp.zeros_like(state)

    def sigma(span, extra):
        level = jnp.full((1, 128), step_ref[span] + extra, jnp.int32).astype(F32)
        frac = 1.0 - level / NSTEPS
        return 3.0 * frac / (1.0 + 2.0 * frac)

    def rdma(src, dst, send, recv, dev):
        return pltpu.make_async_remote_copy(
            src_ref=src, dst_ref=dst, send_sem=send, recv_sem=recv, device_id=dev, device_id_type=MESH
        )

    def drain(ref, sem):
        pltpu.make_async_copy(ref, ref, sem).wait()

    def half_of(n):
        return pl.ds(pl.multiple_of(n * HALF, HALF), HALF)

    pl.semaphore_wait(barrier, 14)
    give = rdma(latent_ref.at[half_of(1 - zhi), :], swap.at[half_of(zhi), :], xs.at[0], xr.at[0], z_peer(4))
    give.start()
    give.wait_recv()
    mine = (lax.broadcasted_iota(jnp.int32, (ROWS, CHANS), 0) < HALF) == (zhi == 0)
    state[:, 0:CHANS] = jnp.where(mine, latent_ref[...], swap[...])
    loads[0].wait()

    def step(s, carry):
        def area(which, blk, count):
            at = pl.multiple_of(blk * HALF, HALF)
            return grid.at[s, which, :, pl.ds(at, count * HALF), :]

        def chunk_of(which, half, o):
            at = pl.multiple_of(o * CHUNK, CHUNK)
            return grid.at[s, which, half, pl.ds(at, CHUNK), :]

        augs = []
        for span in range(4):
            sig = sigma(span, s)
            shi = sig.astype(BF).astype(F32)
            slo = sig - shi
            augs.append(
                jnp.where(
                    (lane == CHANS) | (lane == CHANS + 1),
                    shi,
                    jnp.where(lane == CHANS + 2, slo, jnp.where(lane == CHANS + 3, 1.0, 0.0)),
                )
            )
            aug[span] = jnp.broadcast_to(augs[span], (8, 128))
        patches = state[...]
        own = (patches + jnp.where(low, aug[kind][0:1, :], aug[3 - kind][0:1, :])).astype(BF)

        squares = jnp.zeros((ROWS, 128), F32)
        pk = dot_nn(own, wk[...])
        for h in range(HEADS):
            part = pk[:, h * HD : (h + 1) * HD]
            ms = jnp.sum(part * part, axis=-1, keepdims=True)
            squares = jnp.where((lane == CHANS + h) | (lane == CHANS + HEADS + h), ms, squares)
        factor = gk / jnp.sqrt(squares * (1.0 / HD) + 1e-06)
        fhi = factor.astype(BF).astype(F32)
        row = jnp.where(lane < CHANS, patches, jnp.where(lane < CHANS + HEADS, fhi, factor - fhi)).astype(BF)
        blk = outer * 32 + inner * 8 + z
        mine_at = pl.ds(pl.multiple_of(blk * HALF, HALF), HALF)
        grid[s, kind, 0, mine_at, :] = row[0:HALF]
        grid[s, kind, 1, mine_at, :] = row[HALF:]

        block = area(kind, blk, 1)
        for d in range(1, 8):
            rdma(block, block, zs.at[s], zr.at[s], z_peer(d)).start()

        @pl.when(s == 0)
        def _():
            loads[1].wait()

        pq = dot_nn(own, wq[...])
        normed = []
        for h in range(HEADS):
            part = pq[:, h * HD : (h + 1) * HD]
            ms = jnp.sum(part * part, axis=-1, keepdims=True) * (1.0 / HD)
            normed.append((part / jnp.sqrt(ms + 1e-06) * gain_ref[0, h]).astype(BF))
        for h in range(HEADS):
            flat[pl.ds(h, ROWS, stride=HEADS), :] = dot_nt(normed[h], wk[:, h * HD : (h + 1) * HD])

        drain(area(kind, 0, 7), zr.at[s])
        line = area(kind, outer * 32 + inner * 8, 8)
        for d in range(1, 4):
            rdma(line, line, p2s.at[s], p2r.at[s], inner_peer(d)).start()

        qk = flat[...]
        qhi = qk.astype(BF)
        q2[:, 0:128] = qhi
        q2[:, 128:256] = (qk - qhi.astype(F32)).astype(BF)
        for ref in (acc, accx):
            ref[...] = jnp.zeros_like(ref)
        for ref in (top, topx):
            ref[...] = jnp.full_like(ref, -1e30)

        drain(area(kind, 0, 24), p2r.at[s])
        plane = area(kind, outer * 32, 32)
        for d in (1, 3, 2):
            rdma(plane, plane, p3s.at[s], p3r.at[s, outer], outer_peer(d)).start()

        def share(k):
            @pl.when(kind == 0)
            def _():
                ref = chunk_of(0, 0, (y + k) % 4)
                rdma(ref, ref, cs.at[s], cr.at[s, k], mate).start()

            @pl.when(kind == 1)
            def _():
                ref = area(1, ((x + k) % 4) * 32, 32)
                rdma(ref, ref, cs.at[s], cr.at[s, k], mate).start()

        def shared(k):
            @pl.when(kind == 0)
            def _():
                drain(area(1, 0, 32), cr.at[s, k])

            @pl.when(kind == 1)
            def _():
                drain(chunk_of(0, 0, 0), cr.at[s, k])

        def arrived(k):
            drain(area(kind, 0, 32), p3r.at[s, (outer + k) % 4])

        def attend(k):
            at_a, at_b = (y + k) % 4, (x + k) % 4
            blocks = [
                (0, chunk_of(0, 0, at_a)),
                (1, chunk_of(1, 0, at_b)),
                (2, chunk_of(1, 1, at_b)),
                (3 - 2 * kind, chunk_of(kind, 1 - kind, jnp.where(along_x, at_a, at_b))),
            ]
            keys, factors, turned = [], [], []
            for span, ref in blocks:
                g = ref[...]
                g2 = g * pmask.astype(BF) + aug[span][0:1, :].astype(BF)
                keys.append(jnp.concatenate([g2, g2], axis=1))
                factors.append(dot_nn(g, spread))
                turned.append(dot_nt(eye, g2).astype(BF))
            spare = pl.ds(pl.multiple_of((1 - kind) * COLS, COLS), COLS)
            first, second, whole = slice(0, COLS), slice(COLS, QUERIES), slice(0, COLS)
            units = [
                (0, first, top, acc, first),
                (0, second, top, acc, second),
                (3, spare, topx, accx, whole),
                (1, second, top, acc, second),
                (2, second, top, acc, second),
            ]

            def score(n):
                b, rows = units[n][:2]
                return dot_nt(keys[b], q2[rows, :])

            def soften(n, raw):
                b, _, tref, _, cols = units[n]
                scaled, best = [], None
                for at in range(0, CHUNK, SUB):
                    wide = jnp.concatenate([factors[b][at : at + SUB, :]] * (COLS // 128), axis=1)
                    part = raw[at : at + SUB, :] * wide
                    scaled.append(part)
                    high = jnp.max(part.reshape(SUB // 8, 8, COLS), axis=0)
                    best = high if best is None else jnp.maximum(best, high)
                old = tref[0:1, cols]
                new = jnp.maximum(old, jnp.max(best, axis=0, keepdims=True))
                tref[0:1, cols] = new
                weights = [jnp.exp2(part - new).astype(BF) for part in scaled]
                return n, jnp.concatenate(weights, axis=0), jnp.exp2(old - new)

            def gather(n, weights, alpha):
                b, _, _, aref, cols = units[n]
                aref[:, cols] = aref[:, cols] * alpha + dot_nn(turned[b], weights)

            raw = score(0)
            pending = []
            for n in range(len(units)):
                later = score(n + 1) if n + 1 < len(units) else None
                pending.append(soften(n, raw))
                raw = later
                if len(pending) > LAG:
                    gather(*pending.pop(0))
            for item in pending:
                gather(*item)

        share(0)
        shared(0)

        def group(m, carry):
            attend(m ^ (m // 2))

            @pl.when(m == 0)
            def _():
                arrived(1)
                share(1)
                arrived(3)
                share(3)
                shared(1)

            @pl.when(m == 1)
            def _():
                shared(3)

            @pl.when(m == 2)
            def _():
                arrived(2)
                share(2)
                shared(2)

            return carry

        lax.fori_loop(0, 4, group, 0)

        @pl.when(s == 0)
        def _():
            loads[2].wait()
            loads[3].wait()

        joined = []
        for u in range(2):
            cols = slice(u * COLS, (u + 1) * COLS)
            there = kind == 1 - u
            extra = jnp.where(there, topx[0:1, :], -1e30)
            new = jnp.maximum(top[0:1, cols], extra)
            joined.append(
                acc[:, cols] * jnp.exp2(top[0:1, cols] - new)
                + accx[...] * jnp.where(there, jnp.exp2(extra - new), 0.0)
            )
        sums = jnp.concatenate(joined, axis=1)
        flat[...] = (sums / sums[CHANS + 3 : CHANS + 4, :]).T
        attended = []
        for h in range(HEADS):
            zed = flat[pl.ds(h, ROWS, stride=HEADS), :]
            zed_hi = zed.astype(BF)
            zed_lo = (zed - zed_hi.astype(F32)).astype(BF)
            both = dot_nn(jnp.concatenate([zed_hi, zed_lo], axis=0), wv[:, h * HD : (h + 1) * HD])
            attended.append((both[0:ROWS] + both[ROWS:]).astype(BF))
        velocity = dot_nt(jnp.concatenate(attended, axis=1), wo[...])
        lo_change = sigma(kind, s + 1) - sigma(kind, s)
        hi_change = sigma(3 - kind, s + 1) - sigma(3 - kind, s)
        change = jnp.where(low, lo_change, hi_change)
        state[:, 0:CHANS] = state[:, 0:CHANS] + change[:, 0:CHANS] * velocity
        result[1] = velocity

        drain(area(kind, 0, 7), zs.at[s])
        drain(area(kind, 0, 24), p2s.at[s])
        drain(area(kind, 0, 96), p3s.at[s])

        @pl.when(kind == 0)
        def _():
            drain(grid.at[s, 0, 0], cs.at[s])

        @pl.when(kind == 1)
        def _():
            drain(grid.at[s, 1], cs.at[s])

        return carry

    lax.fori_loop(0, 2, step, 0)
    result[0] = state[:, 0:CHANS]
    give_back = rdma(result.at[:, half_of(1 - zhi), :], back.at[:, half_of(zhi), :], xs.at[1], xr.at[1], z_peer(4))
    give_back.start()
    give_back.wait_recv()
    state_out[...] = jnp.where(mine, result[0], back[0])
    vel_out[...] = jnp.where(mine, result[1], back[1])
    give.wait_send()
    give_back.wait_send()


def local(latent, step_index, w_query, w_key, w_value, cond, qk_gain, w_out):
    vmem = pl.BlockSpec(memory_space=pltpu.VMEM)
    smem = pl.BlockSpec(memory_space=pltpu.SMEM)
    hbm = pl.BlockSpec(memory_space=pl.ANY)
    dma = pltpu.SemaphoreType.DMA
    out = jax.ShapeDtypeStruct((ROWS, CHANS), F32)
    state, velocity = pl.pallas_call(
        kernel,
        out_shape=(out, out),
        in_specs=[smem, smem, vmem, vmem, hbm, hbm, hbm, hbm],
        out_specs=(vmem, vmem),
        scratch_shapes=[
            pltpu.VMEM((2, 2, 2, SEQ, 128), BF),
            pltpu.VMEM((128, WIDTH), BF),
            pltpu.VMEM((128, WIDTH), BF),
            pltpu.VMEM((128, WIDTH), BF),
            pltpu.VMEM((CHANS, WIDTH), BF),
            pltpu.VMEM((4, 8, 128), F32),
            pltpu.VMEM((ROWS, 128), F32),
            pltpu.VMEM((ROWS, CHANS), F32),
            pltpu.VMEM((2, ROWS, CHANS), F32),
            pltpu.VMEM((2, ROWS, CHANS), F32),
            pltpu.VMEM((QUERIES, 256), BF),
            pltpu.VMEM((QUERIES, 128), F32),
            pltpu.VMEM((128, QUERIES), F32),
            pltpu.VMEM((8, QUERIES), F32),
            pltpu.VMEM((128, COLS), F32),
            pltpu.VMEM((8, COLS), F32),
            dma((4,)),
            dma((2,)),
            dma((2,)),
            dma((2,)),
            dma((2,)),
            dma((2,)),
            dma((2, 4)),
            dma((2,)),
            dma((2, 4)),
            dma((2,)),
            dma((2,)),
        ],
        compiler_params=pltpu.CompilerParams(
            collective_id=0, has_side_effects=True, vmem_limit_bytes=63 * 1024 * 1024
        ),
    )(step_index, qk_gain, latent[0], cond, w_query, w_key, w_value, w_out.T)
    return state[None], velocity[None]


def solution(mesh):
    return jax.shard_map(
        local,
        mesh=mesh,
        in_specs=(P("span", "tok", None), P(), P(), P(), P(), P(), P(), P()),
        out_specs=(P("span", "tok", None), P("span", "tok", None)),
        check_vma=False,
    )
```

time: 75.6 us -> 76.2 us (level)
  the two profiles are of different devices: /device:TPU:226 before, /device:TPU:7 now
where the time goes in v2:
time: 76.2 us; the launch traced here: 76 us
  Pallas kernels  73.5 us (96%)
  local copies, waits for them, and re-layouts  1.94 us (3%)
    pallas_call x1, Pallas kernels, local(): pl.pallas_call(kernel, out_shape=(out, out), in_specs=[smem, smem, vmem,...  73.5 us
    unnamed x4, local copies, waits for them, and re-layouts  1.94 us

profile of v2, /device:TPU:7, one launch (start us, length us, event | category | flops | bytes accessed | tf_op | source)
XLA Modules:
  0.0 76.0 jit_solution(684555129537465744)
XLA Ops:
  0.6 73.5 %shard_map.95 = (f32[32,64]{1,0:T(8,128)}, f32[32,64]{1,0:T(8,128)}) custom-call(s32[4]{0:T(128)} %step_ref.1, f32[2,32]{1,0:T(2,128)} %gain_ref.1, f32[32,64]{1,0:T(8,128)} %bitcast.5, f32[3,4096]{1,0:T(4,128)} %cond_ref.1, bf16[64,4096]{1,0:T(8,128)(2,1)} %wq_hbm.1, bf16[64,4096]{1,0:T(8,128)(2,1)} %wk_hbm.1, bf16[64,4096]{1,0:T(8,128)(2,1)} %wv_hbm.1, ...), custom_call_target="tpu_custom_call" | custom-call | tf_op jit(solution)/shard_map/pallas_call | solution.py:385
  74.1 0.0 copy-start
  74.1 1.3 %copy.12 = f32[1,32,64]{2,1,0:T(8,128)} copy(f32[1,32,64]{2,1,0:T(8,128)} %bitcast.7) | data formatting | bytes 16384
  75.4 0.0 copy-done
  75.4 0.6 copy.13
Async XLA Ops:
  74.1 1.3 %copy-start = (f32[32,64]{1,0:T(8,128)S(1)}, f32[32,64]{1,0:T(8,128)}, u32[]{:S(2)}) copy-start(f32[32,64]{1,0:T(8,128)} %get-tuple-element.5) | copy-start | bytes 24580

commit v3 on v1

v3 whole, which is shorter than its diff:
```python
import jax
import jax.numpy as jnp
from jax import lax
from jax.experimental import pallas as pl
from jax.experimental.pallas import tpu as pltpu
from jax.sharding import PartitionSpec as P

MESH = pl.DeviceIdType.MESH
NSTEPS = 8
ROWS = 32
PIECE = 4 * ROWS
CHANS = 64
HEADS = 32
HD = 128
WIDTH = HEADS * HD
SEQ = 2048
CHUNK = SEQ // 4
QUERIES = HEADS * ROWS
COLS = QUERIES // 2
SUB = 64
LAG = 2
PLACES = (
    (0, 0), (1, 0), (3, 0), (0, 1), (0, 3), (1, 1), (3, 3), (1, 3),
    (3, 1), (2, 0), (0, 2), (2, 1), (2, 3), (1, 2), (3, 2), (2, 2),
)
SLOT = {place: n for n, place in enumerate(PLACES)}
LOG2E = 1.4426950408889634
BF = jnp.bfloat16
F32 = jnp.float32


def dot_nt(a, b):
    return lax.dot_general(a, b, (((1,), (1,)), ((), ())), preferred_element_type=F32)


def dot_nn(a, b):
    return jnp.dot(a, b, preferred_element_type=F32)


def kernel(
    step_ref, gain_ref, latent_ref, cond_ref, wq_hbm, wk_hbm, wv_hbm, wo_hbm,
    state_out, vel_out,
    grid, wq, wk, wv, wo, aug, state, q2, flat, acc, top,
    wsem, zs, zr, ps, pr, cs, cr,
):
    c = lax.axis_index("span")
    t = lax.axis_index("tok")
    zhi = c // 2
    core = c % 2
    y = t // 16
    zl = (t // 4) % 4
    x = t % 4
    upper = zhi == 1

    def tok(yy, zz, xx):
        return yy * 16 + zz * 4 + xx

    def plane_peer(place):
        return c, tok((y + place[0]) % 4, zl, (x + place[1]) % 4)

    across_z = (1 - zhi) * 2 + core
    mate = (zhi * 2 + 1 - core, t)

    loads = [
        pltpu.make_async_copy(wk_hbm, wk.at[pl.ds(0, CHANS), :], wsem.at[0]),
        pltpu.make_async_copy(wq_hbm, wq.at[pl.ds(0, CHANS), :], wsem.at[1]),
        pltpu.make_async_copy(wv_hbm, wv.at[pl.ds(0, CHANS), :], wsem.at[2]),
        pltpu.make_async_copy(wo_hbm, wo, wsem.at[3]),
    ]
    for item in loads:
        item.start()

    barrier = pltpu.get_barrier_semaphore()

    def greet(dev):
        pl.semaphore_signal(barrier, inc=1, device_id=dev, device_id_type=MESH)

    for d in range(1, 4):
        greet((c, tok(y, (zl + d) % 4, x)))
    for d in range(4):
        greet((across_z, tok(y, d, x)))
    for place in PLACES[1:]:
        greet(plane_peer(place))
    greet(mate)

    lane = lax.broadcasted_iota(jnp.int32, (1, 128), 1)
    row16 = lax.broadcasted_iota(jnp.int32, (16, WIDTH), 0)
    for which, ref in enumerate((wq, wk, wv)):
        cvec = cond_ref[which : which + 1, :]
        chi = cvec.astype(BF).astype(F32)
        clo = cvec - chi
        rows = jnp.where((row16 == 0) | (row16 == 2), chi, jnp.where(row16 == 1, clo, 0.0))
        ref[CHANS : CHANS + 16, :] = rows.astype(BF)
        ref[CHANS + 16 :, :] = jnp.zeros((128 - CHANS - 16, WIDTH), BF)
    gk = jnp.zeros((1, 128), F32)
    for h in range(HEADS):
        gk = jnp.where((lane == CHANS + h) | (lane == CHANS + HEADS + h), gain_ref[1, h], gk)
    gk = gk * (HD ** (-0.5) * LOG2E)
    down = lax.broadcasted_iota(jnp.int32, (128, 128), 0)
    across = lax.broadcasted_iota(jnp.int32, (128, 128), 1)
    spread = jnp.where((down >= CHANS) & (down % HEADS == across % HEADS), 1.0, 0.0).astype(BF)
    eye = jnp.where(down == across, 1.0, 0.0).astype(BF)
    pmask = jnp.where(lane < CHANS, 1.0, 0.0)
    state[...] = jnp.zeros_like(state)
    state[:, 0:CHANS] = latent_ref[...]

    def sigma(span, extra):
        level = jnp.full((1, 128), step_ref[span] + extra, jnp.int32).astype(F32)
        frac = 1.0 - level / NSTEPS
        return 3.0 * frac / (1.0 + 2.0 * frac)

    def rdma(src, dst, send, recv, dev):
        return pltpu.make_async_remote_copy(
            src_ref=src, dst_ref=dst, send_sem=send, recv_sem=recv, device_id=dev, device_id_type=MESH
        )

    def drain(ref, sem):
        pltpu.make_async_copy(ref, ref, sem).wait()

    loads[0].wait()

    def step(s, carry):
        def rows_of(e, at, count):
            return grid.at[s, e, pl.ds(at, count), :]

        def chunk_of(e, g):
            at = pl.multiple_of(g * CHUNK, CHUNK)
            return grid.at[s, e, pl.ds(at, CHUNK), :]

        for span in range(4):
            sig = sigma(span, s)
            shi = sig.astype(BF).astype(F32)
            slo = sig - shi
            line = jnp.where(
                (lane == CHANS) | (lane == CHANS + 1),
                shi,
                jnp.where(lane == CHANS + 2, slo, jnp.where(lane == CHANS + 3, 1.0, 0.0)),
            )
            aug[span] = jnp.broadcast_to(line, (8, 128))
        patches = state[...]
        own = (patches + aug[c][0:1, :]).astype(BF)

        squares = jnp.zeros((ROWS, 128), F32)
        pk = dot_nn(own, wk[...])
        for h in range(HEADS):
            part = pk[:, h * HD : (h + 1) * HD]
            ms = jnp.sum(part * part, axis=-1, keepdims=True)
            squares = jnp.where((lane == CHANS + h) | (lane == CHANS + HEADS + h), ms, squares)
        factor = gk / jnp.sqrt(squares * (1.0 / HD) + 1e-06)
        fhi = factor.astype(BF).astype(F32)
        row = jnp.where(lane < CHANS, patches, jnp.where(lane < CHANS + HEADS, fhi, factor - fhi)).astype(BF)
        at = pl.multiple_of(zl * ROWS, ROWS)
        grid[s, c, pl.ds(at, ROWS), :] = row

        @pl.when(s == 0)
        def _():
            pl.semaphore_wait(barrier, 23)

        block = rows_of(c, at, ROWS)
        for d in range(1, 4):
            rdma(block, block, zs.at[s], zr.at[s, zhi], (c, tok(y, (zl + d) % 4, x))).start()

        @pl.when(jnp.logical_not(upper))
        def _():
            for d in range(4):
                rdma(block, block, zs.at[s], zr.at[s, 0], (across_z, tok(y, d, x))).start()

        def spread_plane(ss, r):
            e = core + 2 * r
            for place in PLACES[1:]:
                slot = SLOT[(-place[0] % 4, -place[1] % 4)]
                rdma(
                    grid.at[ss, e, pl.ds(0, PIECE), :],
                    grid.at[ss, e, pl.ds(slot * PIECE, PIECE), :],
                    ps.at[ss, r],
                    pr.at[ss, r, slot // 4],
                    plane_peer(place),
                ).start()

        def own_plane():
            drain(rows_of(0, 0, 3 * ROWS), zr.at[s, zhi])
            spread_plane(s, zhi)

        def lower_plane(ss):
            drain(rows_of(0, 0, 4 * ROWS), zr.at[ss, 0])
            spread_plane(ss, 0)

        @pl.when(s == 0)
        def _():
            loads[1].wait()

        pq = dot_nn(own, wq[...])
        normed = []
        for h in range(HEADS):
            part = pq[:, h * HD : (h + 1) * HD]
            ms = jnp.sum(part * part, axis=-1, keepdims=True) * (1.0 / HD)
            normed.append((part / jnp.sqrt(ms + 1e-06) * gain_ref[0, h]).astype(BF))
        for h in range(HEADS):
            flat[pl.ds(h, ROWS, stride=HEADS), :] = dot_nt(normed[h], wk[:, h * HD : (h + 1) * HD])
        qk = flat[...]
        qhi = qk.astype(BF)
        q2[:, 0:128] = qhi
        q2[:, 128:256] = (qk - qhi.astype(F32)).astype(BF)
        acc[...] = jnp.zeros_like(acc)
        top[...] = jnp.full_like(top, -1e30)
        late = (s == 1) & (c == 3)

        @pl.when(jnp.logical_not(late))
        def _():
            own_plane()

        @pl.when(upper & (s == 0))
        def _():
            lower_plane(0)

        def attend(blocks):
            keys, factors, turned = [], [], []
            for e, g in blocks:
                rows = chunk_of(e, g)[...]
                plain = rows * pmask.astype(BF) + aug[e][0:1, :].astype(BF)
                keys.append(jnp.concatenate([plain, plain], axis=1))
                factors.append(dot_nn(rows, spread))
                turned.append(dot_nt(eye, plain).astype(BF))
            units = [(b, slice(u * COLS, (u + 1) * COLS)) for b in range(len(blocks)) for u in range(QUERIES // COLS)]

            def score(n):
                b, cols = units[n]
                return dot_nt(keys[b], q2[cols, :])

            def soften(n, raw):
                b, cols = units[n]
                scaled, best = [], None
                for at in range(0, CHUNK, SUB):
                    wide = jnp.concatenate([factors[b][at : at + SUB, :]] * (COLS // 128), axis=1)
                    part = raw[at : at + SUB, :] * wide
                    scaled.append(part)
                    high = jnp.max(part.reshape(SUB // 8, 8, COLS), axis=0)
                    best = high if best is None else jnp.maximum(best, high)
                old = top[0:1, cols]
                new = jnp.maximum(old, jnp.max(best, axis=0, keepdims=True))
                top[0:1, cols] = new
                weights = [jnp.exp2(part - new).astype(BF) for part in scaled]
                return n, jnp.concatenate(weights, axis=0), jnp.exp2(old - new)

            def gather(n, weights, alpha):
                b, cols = units[n]
                acc[:, cols] = acc[:, cols] * alpha + dot_nn(turned[b], weights)

            raw = score(0)
            pending = []
            for n in range(len(units)):
                later = score(n + 1) if n + 1 < len(units) else None
                pending.append(soften(n, raw))
                raw = later
                if len(pending) > LAG:
                    gather(*pending.pop(0))
            for item in pending:
                gather(*item)

        three = (s == 0) & (c == 2)
        count = jnp.where(three, 3, 4)

        def place_of(m, q):
            e = jnp.where(s == 0, jnp.where(three, q, q % (c + 1)), m)
            g = jnp.where(s == 0, jnp.where(three, m, (4 * m + q) // (c + 1)), q)
            return e, g

        def group(m, carry):
            def arrive(q, carry):
                e, g = place_of(m, q)
                r = e // 2

                @pl.when(e % 2 == core)
                def _():
                    @pl.when(g == 0)
                    def _():
                        drain(rows_of(0, 0, 3 * PIECE), pr.at[s, r, g])

                    @pl.when(g > 0)
                    def _():
                        drain(rows_of(0, 0, 4 * PIECE), pr.at[s, r, g])

                    @pl.when(r <= zhi - core)
                    def _():
                        ref = chunk_of(e, g)
                        rdma(ref, ref, cs.at[s, r], cr.at[s, r, g], mate).start()

                return carry

            def cross(q, carry):
                e, g = place_of(m, q)

                @pl.when(e % 2 != core)
                def _():
                    drain(rows_of(0, 0, CHUNK), cr.at[s, e // 2, g])

                return carry

            lax.fori_loop(0, count, arrive, 0)
            lax.fori_loop(0, count, cross, 0)

            @pl.when(three)
            def _():
                attend([place_of(m, q) for q in range(3)])

            @pl.when(jnp.logical_not(three))
            def _():
                attend([place_of(m, q) for q in range(4)])

            @pl.when(late & (m == 0))
            def _():
                own_plane()

            return carry

        lax.fori_loop(0, jnp.where(three, 4, c + 1), group, 0)

        @pl.when(upper & (s == 0))
        def _():
            lower_plane(1)

        @pl.when(s == 0)
        def _():
            loads[2].wait()
            loads[3].wait()

        sums = acc[...]
        flat[...] = (sums / sums[CHANS + 3 : CHANS + 4, :]).T
        attended = []
        for h in range(HEADS):
            zed = flat[pl.ds(h, ROWS, stride=HEADS), :]
            zed_hi = zed.astype(BF)
            zed_lo = (zed - zed_hi.astype(F32)).astype(BF)
            both = dot_nn(jnp.concatenate([zed_hi, zed_lo], axis=0), wv[:, h * HD : (h + 1) * HD])
            attended.append((both[0:ROWS] + both[ROWS:]).astype(BF))
        velocity = dot_nt(jnp.concatenate(attended, axis=1), wo[...])
        change = sigma(c, s + 1) - sigma(c, s)
        state[:, 0:CHANS] = state[:, 0:CHANS] + change[:, 0:CHANS] * velocity
        vel_out[...] = velocity
        return carry

    lax.fori_loop(0, 2, step, 0)
    state_out[...] = state[:, 0:CHANS]

    def finish(s, carry):
        @pl.when(upper)
        def _():
            drain(grid.at[0, 0, pl.ds(0, 3 * ROWS), :], zs.at[s])

        @pl.when(jnp.logical_not(upper))
        def _():
            drain(grid.at[0, 0, pl.ds(0, 7 * ROWS), :], zs.at[s])

        def rail(r, carry):
            drain(grid.at[0, 0, pl.ds(0, 15 * PIECE), :], ps.at[s, r])

            @pl.when(r <= zhi - core)
            def _():
                drain(grid.at[0, 0], cs.at[s, r])

            return carry

        lax.fori_loop(0, zhi + 1, rail, 0)
        return carry

    lax.fori_loop(0, 2, finish, 0)


def local(latent, step_index, w_query, w_key, w_value, cond, qk_gain, w_out):
    vmem = pl.BlockSpec(memory_space=pltpu.VMEM)
    smem = pl.BlockSpec(memory_space=pltpu.SMEM)
    hbm = pl.BlockSpec(memory_space=pl.ANY)
    dma = pltpu.SemaphoreType.DMA
    out = jax.ShapeDtypeStruct((ROWS, CHANS), F32)
    state, velocity = pl.pallas_call(
        kernel,
        out_shape=(out, out),
        in_specs=[smem, smem, vmem, vmem, hbm, hbm, hbm, hbm],
        out_specs=(vmem, vmem),
        scratch_shapes=[
            pltpu.VMEM((2, 4, SEQ, 128), BF),
            pltpu.VMEM((128, WIDTH), BF),
            pltpu.VMEM((128, WIDTH), BF),
            pltpu.VMEM((128, WIDTH), BF),
            pltpu.VMEM((CHANS, WIDTH), BF),
            pltpu.VMEM((4, 8, 128), F32),
            pltpu.VMEM((ROWS, 128), F32),
            pltpu.VMEM((QUERIES, 256), BF),
            pltpu.VMEM((QUERIES, 128), F32),
            pltpu.VMEM((128, QUERIES), F32),
            pltpu.VMEM((8, QUERIES), F32),
            dma((4,)),
            dma((2,)),
            dma((2, 2)),
            dma((2, 2)),
            dma((2, 2, 4)),
            dma((2, 2)),
            dma((2, 2, 4)),
        ],
        compiler_params=pltpu.CompilerParams(
            collective_id=0, has_side_effects=True, vmem_limit_bytes=63 * 1024 * 1024
        ),
    )(step_index, qk_gain, latent[0], cond, w_query, w_key, w_value, w_out.T)
    return state[None], velocity[None]


def solution(mesh):
    return jax.shard_map(
        local,
        mesh=mesh,
        in_specs=(P("span", "tok", None), P(), P(), P(), P(), P(), P(), P()),
        out_specs=(P("span", "tok", None), P("span", "tok", None)),
        check_vma=False,
    )
```

time: 75.6 us -> 66.5 us (0.88)
  the two profiles are of different devices: /device:TPU:226 before, /device:TPU:225 now
where the time goes in v3:
time: 66.5 us; the launch traced here: 66.3 us
  Pallas kernels  63.8 us (96%)
  local copies, waits for them, and re-layouts  1.94 us (3%)
    pallas_call x1, Pallas kernels, local(): pl.pallas_call(kernel, out_shape=(out, out), in_specs=[smem, smem, vmem,...  63.8 us
    unnamed x4, local copies, waits for them, and re-layouts  1.94 us

profile of v3, /device:TPU:225, one launch (start us, length us, event | category | flops | bytes accessed | tf_op | source)
XLA Modules:
  0.0 66.3 jit_solution(13582785739329672566)
XLA Ops:
  0.6 63.8 %shard_map.95 = (f32[32,64]{1,0:T(8,128)}, f32[32,64]{1,0:T(8,128)}) custom-call(s32[4]{0:T(128)} %step_ref.1, f32[2,32]{1,0:T(2,128)} %gain_ref.1, f32[32,64]{1,0:T(8,128)} %bitcast.5, f32[3,4096]{1,0:T(4,128)} %cond_ref.1, bf16[64,4096]{1,0:T(8,128)(2,1)} %wq_hbm.1, bf16[64,4096]{1,0:T(8,128)(2,1)} %wk_hbm.1, bf16[64,4096]{1,0:T(8,128)(2,1)} %wv_hbm.1, ...), custom_call_target="tpu_custom_call" | custom-call | tf_op jit(solution)/shard_map/pallas_call | solution.py:375
  64.4 0.0 copy-start
  64.4 1.3 %copy.12 = f32[1,32,64]{2,1,0:T(8,128)} copy(f32[1,32,64]{2,1,0:T(8,128)} %bitcast.7) | data formatting | bytes 16384
  65.7 0.0 copy-done
  65.7 0.6 copy.13
Async XLA Ops:
  64.4 1.3 %copy-start = (f32[32,64]{1,0:T(8,128)S(1)}, f32[32,64]{1,0:T(8,128)}, u32[]{:S(2)}) copy-start(f32[32,64]{1,0:T(8,128)} %get-tuple-element.5) | copy-start | bytes 24580

commit v4 on v3

--- a/solution.py
+++ b/solution.py
@@ -23,7 +23,27 @@
     (0, 0), (1, 0), (3, 0), (0, 1), (0, 3), (1, 1), (3, 3), (1, 3),
     (3, 1), (2, 0), (0, 2), (2, 1), (2, 3), (1, 2), (3, 2), (2, 2),
 )
-SLOT = {place: n for n, place in enumerate(PLACES)}
+WHOLE = [[(e, g) for g in range(4)] for e in range(4)]
+GROUPS = (
+    (
+        [[(0, 0), (0, 1)], [(0, 2), (0, 3)]],
+        [[(1, 0), (1, 1), (0, 0), (0, 1)], [(1, 2), (1, 3), (0, 2), (0, 3)]],
+        [[(2, 0), (0, 0), (2, 1), (0, 1)], [(2, 2), (0, 2), (1, 0), (1, 1)], [(2, 3), (0, 3), (1, 2), (1, 3)]],
+        [
+            [(3, 0), (1, 0), (3, 1), (1, 1)],
+            [(2, 0), (0, 0), (2, 1), (0, 1)],
+            [(3, 2), (1, 2), (2, 2), (0, 2)],
+            [(3, 3), (1, 3), (2, 3), (0, 3)],
+        ],
+    ),
+    (
+        [[(0, 0), (0, 1)], [(0, 2), (0, 3)]],
+        [WHOLE[0], WHOLE[1]],
+        [WHOLE[0], WHOLE[1], WHOLE[2]],
+        [WHOLE[0], WHOLE[1], [(3, 0), (3, 1), (2, 0), (2, 1)], [(3, 2), (3, 3), (2, 2), (2, 3)]],
+    ),
+)
+AHEAD = {(1, 2, 1): [(2, 0), (2, 1)]}
 LOG2E = 1.4426950408889634
 BF = jnp.bfloat16
 F32 = jnp.float32
@@ -39,24 +59,24 @@
 
 def kernel(
     step_ref, gain_ref, latent_ref, cond_ref, wq_hbm, wk_hbm, wv_hbm, wo_hbm,
-    state_out, vel_out,
+    out_ref,
     grid, wq, wk, wv, wo, aug, state, q2, flat, acc, top,
     wsem, zs, zr, ps, pr, cs, cr,
 ):
     c = lax.axis_index("span")
     t = lax.axis_index("tok")
-    zhi = c // 2
-    core = c % 2
-    y = t // 16
-    zl = (t // 4) % 4
-    x = t % 4
+    zhi = c >> 1
+    core = c & 1
+    y = t >> 4
+    zl = (t >> 2) & 3
+    x = t & 3
     upper = zhi == 1
 
     def tok(yy, zz, xx):
-        return yy * 16 + zz * 4 + xx
+        return (yy << 4) | (zz << 2) | xx
 
     def plane_peer(place):
-        return c, tok((y + place[0]) % 4, zl, (x + place[1]) % 4)
+        return c, tok((y + place[0]) & 3, zl, (x + place[1]) & 3)
 
     across_z = (1 - zhi) * 2 + core
     mate = (zhi * 2 + 1 - core, t)
@@ -76,7 +96,7 @@
         pl.semaphore_signal(barrier, inc=1, device_id=dev, device_id_type=MESH)
 
     for d in range(1, 4):
-        greet((c, tok(y, (zl + d) % 4, x)))
+        greet((c, tok(y, (zl + d) & 3, x)))
     for d in range(4):
         greet((across_z, tok(y, d, x)))
     for place in PLACES[1:]:
@@ -158,32 +178,33 @@
 
         block = rows_of(c, at, ROWS)
         for d in range(1, 4):
-            rdma(block, block, zs.at[s], zr.at[s, zhi], (c, tok(y, (zl + d) % 4, x))).start()
+            rdma(block, block, zs.at[s], zr.at[s, zhi], (c, tok(y, (zl + d) & 3, x))).start()
 
         @pl.when(jnp.logical_not(upper))
         def _():
             for d in range(4):
                 rdma(block, block, zs.at[s], zr.at[s, 0], (across_z, tok(y, d, x))).start()
 
-        def spread_plane(ss, r):
+        def send_chunk(ss, r, g):
             e = core + 2 * r
-            for place in PLACES[1:]:
-                slot = SLOT[(-place[0] % 4, -place[1] % 4)]
+            for slot in range(max(4 * g, 1), 4 * g + 4):
                 rdma(
                     grid.at[ss, e, pl.ds(0, PIECE), :],
                     grid.at[ss, e, pl.ds(slot * PIECE, PIECE), :],
-                    ps.at[ss, r],
-                    pr.at[ss, r, slot // 4],
-                    plane_peer(place),
+                    ps.at[ss, r, g],
+                    pr.at[ss, r, g],
+                    plane_peer((-PLACES[slot][0], -PLACES[slot][1])),
                 ).start()
 
         def own_plane():
             drain(rows_of(0, 0, 3 * ROWS), zr.at[s, zhi])
-            spread_plane(s, zhi)
+            for g in range(4):
+                send_chunk(s, zhi, g)
 
         def lower_plane(ss):
             drain(rows_of(0, 0, 4 * ROWS), zr.at[ss, 0])
-            spread_plane(ss, 0)
+            for g in range(4):
+                send_chunk(ss, 0, g)
 
         @pl.when(s == 0)
         def _():
@@ -203,15 +224,17 @@
         q2[:, 128:256] = (qk - qhi.astype(F32)).astype(BF)
         acc[...] = jnp.zeros_like(acc)
         top[...] = jnp.full_like(top, -1e30)
-        late = (s == 1) & (c == 3)
-
-        @pl.when(jnp.logical_not(late))
+        @pl.when(jnp.logical_not(upper) | (s == 1))
         def _():
             own_plane()
 
         @pl.when(upper & (s == 0))
         def _():
-            lower_plane(0)
+            drain(rows_of(0, 0, 3 * ROWS), zr.at[s, 1])
+            drain(rows_of(0, 0, 4 * ROWS), zr.at[s, 0])
+            for g in range(4):
+                for r in range(2):
+                    send_chunk(s, r, g)
 
         def attend(blocks):
             keys, factors, turned = [], [], []
@@ -257,65 +280,48 @@
             for item in pending:
                 gather(*item)
 
-        three = (s == 0) & (c == 2)
-        count = jnp.where(three, 3, 4)
-
-        def place_of(m, q):
-            e = jnp.where(s == 0, jnp.where(three, q, q % (c + 1)), m)
-            g = jnp.where(s == 0, jnp.where(three, m, (4 * m + q) // (c + 1)), q)
-            return e, g
-
         def group(m, carry):
-            def arrive(q, carry):
-                e, g = place_of(m, q)
-                r = e // 2
-
-                @pl.when(e % 2 == core)
-                def _():
-                    @pl.when(g == 0)
-                    def _():
-                        drain(rows_of(0, 0, 3 * PIECE), pr.at[s, r, g])
-
-                    @pl.when(g > 0)
-                    def _():
-                        drain(rows_of(0, 0, 4 * PIECE), pr.at[s, r, g])
-
-                    @pl.when(r <= zhi - core)
-                    def _():
-                        ref = chunk_of(e, g)
-                        rdma(ref, ref, cs.at[s, r], cr.at[s, r, g], mate).start()
-
-                return carry
-
-            def cross(q, carry):
-                e, g = place_of(m, q)
-
-                @pl.when(e % 2 != core)
-                def _():
-                    drain(rows_of(0, 0, CHUNK), cr.at[s, e // 2, g])
-
-                return carry
-
-            lax.fori_loop(0, count, arrive, 0)
-            lax.fori_loop(0, count, cross, 0)
-
-            @pl.when(three)
+            key = s * 16 + c * 4 + m
+            code = jnp.int32(0)
+            for ss in range(2):
+                for cc in range(4):
+                    for mm, chunks in enumerate(GROUPS[ss][cc]):
+                        here = key == ss * 16 + cc * 4 + mm
+                        packed = sum((4 * e + g) << (4 * q) for q, (e, g) in enumerate(chunks))
+                        code = jnp.where(here, packed, code)
+
+                        @pl.when(here)
+                        def _(ss=ss, cc=cc, mm=mm, chunks=chunks):
+                            for e, g in chunks + AHEAD.get((ss, cc, mm), []):
+                                r = e // 2
+                                if e % 2 == cc % 2 and (e, g) not in AHEAD.get((ss, cc, mm - 1), []):
+                                    drain(rows_of(0, 0, (4 if g else 3) * PIECE), pr.at[ss, r, g])
+                                    if r <= cc // 2 - cc % 2:
+                                        ref = grid.at[ss, e, pl.ds(g * CHUNK, CHUNK), :]
+                                        rdma(ref, ref, cs.at[ss, r], cr.at[ss, r, g], mate).start()
+                            for e, g in chunks:
+                                if e % 2 != cc % 2:
+                                    drain(rows_of(0, 0, CHUNK), cr.at[ss, e // 2, g])
+
+            @pl.when((s == 0) & (c == 2) & (m == 2))
             def _():
-                attend([place_of(m, q) for q in range(3)])
-
-            @pl.when(jnp.logical_not(three))
+                lower_plane(1)
+
+            blocks = [((code >> (4 * q + 2)) & 3, (code >> (4 * q)) & 3) for q in range(4)]
+
+            @pl.when(c == 0)
             def _():
-                attend([place_of(m, q) for q in range(4)])
-
-            @pl.when(late & (m == 0))
+                attend(blocks[:2])
+
+            @pl.when(c > 0)
             def _():
-                own_plane()
+                attend(blocks)
 
             return carry
 
-        lax.fori_loop(0, jnp.where(three, 4, c + 1), group, 0)
-
-        @pl.when(upper & (s == 0))
+        lax.fori_loop(0, jnp.maximum(c + 1, 2), group, 0)
+
+        @pl.when((s == 0) & (c == 3))
         def _():
             lower_plane(1)
 
@@ -336,11 +342,11 @@
         velocity = dot_nt(jnp.concatenate(attended, axis=1), wo[...])
         change = sigma(c, s + 1) - sigma(c, s)
         state[:, 0:CHANS] = state[:, 0:CHANS] + change[:, 0:CHANS] * velocity
-        vel_out[...] = velocity
+        out_ref[1] = velocity
         return carry
 
     lax.fori_loop(0, 2, step, 0)
-    state_out[...] = state[:, 0:CHANS]
+    out_ref[0] = state[:, 0:CHANS]
 
     def finish(s, carry):
         @pl.when(upper)
@@ -352,7 +358,8 @@
             drain(grid.at[0, 0, pl.ds(0, 7 * ROWS), :], zs.at[s])
 
         def rail(r, carry):
-            drain(grid.at[0, 0, pl.ds(0, 15 * PIECE), :], ps.at[s, r])
+            for g in range(4):
+                drain(grid.at[0, 0, pl.ds(0, (4 if g else 3) * PIECE), :], ps.at[s, r, g])
 
             @pl.when(r <= zhi - core)
             def _():
@@ -371,12 +378,11 @@
     smem = pl.BlockSpec(memory_space=pltpu.SMEM)
     hbm = pl.BlockSpec(memory_space=pl.ANY)
     dma = pltpu.SemaphoreType.DMA
-    out = jax.ShapeDtypeStruct((ROWS, CHANS), F32)
-    state, velocity = pl.pallas_call(
+    both = pl.pallas_call(
         kernel,
-        out_shape=(out, out),
+        out_shape=jax.ShapeDtypeStruct((2, ROWS, CHANS), F32),
         in_specs=[smem, smem, vmem, vmem, hbm, hbm, hbm, hbm],
-        out_specs=(vmem, vmem),
+        out_specs=vmem,
         scratch_shapes=[
             pltpu.VMEM((2, 4, SEQ, 128), BF),
             pltpu.VMEM((128, WIDTH), BF),
@@ -392,7 +398,7 @@
             dma((4,)),
             dma((2,)),
             dma((2, 2)),
-            dma((2, 2)),
+            dma((2, 2, 4)),
             dma((2, 2, 4)),
             dma((2, 2)),
             dma((2, 2, 4)),
@@ -401,7 +407,7 @@
             collective_id=0, has_side_effects=True, vmem_limit_bytes=63 * 1024 * 1024
         ),
     )(step_index, qk_gain, latent[0], cond, w_query, w_key, w_value, w_out.T)
-    return state[None], velocity[None]
+    return both[0:1], both[1:2]
 
 
 def solution(mesh):

time: 66.5 us -> 57.2 us (0.86)
  the two profiles are of different devices: /device:TPU:225 before, /device:TPU:193 now
where the time goes in v4:
time: 57.2 us; the launch traced here: 57 us
  Pallas kernels  55 us (96%)
  local copies, waits for them, and re-layouts  1.35 us (2%)
  between operations  0.64 us (1%)
    pallas_call x1, Pallas kernels, local(): pl.pallas_call(kernel, out_shape=jax.ShapeDtypeStruct((2, ROWS, CHANS), F...  55 us
    slice x1, local copies, waits for them, and re-layouts, local(): return (both[0:1], both[1:2])  1.35 us

profile of v4, /device:TPU:193, one launch (start us, length us, event | category | flops | bytes accessed | tf_op | source)
XLA Modules:
  0.0 57.0 jit_solution(11851271480335262874)
XLA Ops:
  0.6 55.0 %shard_map.95 = f32[2,32,64]{2,1,0:T(8,128)} custom-call(s32[4]{0:T(128)} %step_ref.1, f32[2,32]{1,0:T(2,128)} %gain_ref.1, f32[32,64]{1,0:T(8,128)} %bitcast.3, f32[3,4096]{1,0:T(4,128)} %cond_ref.1, bf16[64,4096]{1,0:T(8,128)(2,1)} %wq_hbm.1, bf16[64,4096]{1,0:T(8,128)(2,1)} %wk_hbm.1, bf16[64,4096]{1,0:T(8,128)(2,1)} %wv_hbm.1, bf16[64,4096]{1,0:T(8,128)(2,1)} %bitcast.2), custom_call_target="tpu_custom_call" | custom-call | tf_op jit(solution)/shard_map/pallas_call | solution.py:381
  55.6 1.3 %fusion = (f32[1,32,64]{2,1,0:T(8,128)}, f32[1,32,64]{2,1,0:T(8,128)}) fusion(f32[2,32,64]{2,1,0:T(8,128)} %shard_map.95), kind=kLoop, calls=%fused_computation | loop fusion | bytes 32768 | tf_op jit(solution)/shard_map/slice | solution.py:410

commit v5 on v4

--- a/solution.py
+++ b/solution.py
@@ -16,9 +16,9 @@
 SEQ = 2048
 CHUNK = SEQ // 4
 QUERIES = HEADS * ROWS
-COLS = QUERIES // 2
+COLS = QUERIES // 4
 SUB = 64
-LAG = 2
+LAG = 3
 PLACES = (
     (0, 0), (1, 0), (3, 0), (0, 1), (0, 3), (1, 1), (3, 3), (1, 3),
     (3, 1), (2, 0), (0, 2), (2, 1), (2, 3), (1, 2), (3, 2), (2, 2),
@@ -39,11 +39,11 @@
     (
         [[(0, 0), (0, 1)], [(0, 2), (0, 3)]],
         [WHOLE[0], WHOLE[1]],
-        [WHOLE[0], WHOLE[1], WHOLE[2]],
-        [WHOLE[0], WHOLE[1], [(3, 0), (3, 1), (2, 0), (2, 1)], [(3, 2), (3, 3), (2, 2), (2, 3)]],
+        [WHOLE[0], WHOLE[1], [(2, 0), (2, 1)], [(2, 2), (2, 3)]],
+        [WHOLE[1], WHOLE[0], [(3, 0), (3, 1), (2, 0), (2, 1)], [(3, 2), (2, 2)], [(3, 3), (2, 3)]],
     ),
 )
-AHEAD = {(1, 2, 1): [(2, 0), (2, 1)]}
+AHEAD = {(1, 2, 1): [(2, 0), (2, 1)], (1, 2, 2): [(2, 2), (2, 3)]}
 LOG2E = 1.4426950408889634
 BF = jnp.bfloat16
 F32 = jnp.float32
@@ -58,9 +58,9 @@
 
 
 def kernel(
-    step_ref, gain_ref, latent_ref, cond_ref, wq_hbm, wk_hbm, wv_hbm, wo_hbm,
+    step_ref, gain_ref, latent_hbm, cond_hbm, wq_hbm, wk_hbm, wv_hbm, wo_hbm,
     out_ref,
-    grid, wq, wk, wv, wo, aug, state, q2, flat, acc, top,
+    grid, latent_ref, cond_ref, wq, wk, wv, wo, aug, state, q2, flat, acc, top,
     wsem, zs, zr, ps, pr, cs, cr,
 ):
     c = lax.axis_index("span")
@@ -81,15 +81,6 @@
     across_z = (1 - zhi) * 2 + core
     mate = (zhi * 2 + 1 - core, t)
 
-    loads = [
-        pltpu.make_async_copy(wk_hbm, wk.at[pl.ds(0, CHANS), :], wsem.at[0]),
-        pltpu.make_async_copy(wq_hbm, wq.at[pl.ds(0, CHANS), :], wsem.at[1]),
-        pltpu.make_async_copy(wv_hbm, wv.at[pl.ds(0, CHANS), :], wsem.at[2]),
-        pltpu.make_async_copy(wo_hbm, wo, wsem.at[3]),
-    ]
-    for item in loads:
-        item.start()
-
     barrier = pltpu.get_barrier_semaphore()
 
     def greet(dev):
@@ -103,7 +94,19 @@
         greet(plane_peer(place))
     greet(mate)
 
+    loads = [
+        pltpu.make_async_copy(wk_hbm, wk.at[pl.ds(0, CHANS), :], wsem.at[0]),
+        pltpu.make_async_copy(wq_hbm, wq.at[pl.ds(0, CHANS), :], wsem.at[1]),
+        pltpu.make_async_copy(wv_hbm, wv.at[pl.ds(0, CHANS), :], wsem.at[2]),
+        pltpu.make_async_copy(wo_hbm, wo, wsem.at[3]),
+        pltpu.make_async_copy(cond_hbm, cond_ref, wsem.at[4]),
+        pltpu.make_async_copy(latent_hbm, latent_ref, wsem.at[5]),
+    ]
+    for n in (4, 0, 5, 1, 2, 3):
+        loads[n].start()
+
     lane = lax.broadcasted_iota(jnp.int32, (1, 128), 1)
+    loads[4].wait()
     row16 = lax.broadcasted_iota(jnp.int32, (16, WIDTH), 0)
     for which, ref in enumerate((wq, wk, wv)):
         cvec = cond_ref[which : which + 1, :]
@@ -122,6 +125,7 @@
     eye = jnp.where(down == across, 1.0, 0.0).astype(BF)
     pmask = jnp.where(lane < CHANS, 1.0, 0.0)
     state[...] = jnp.zeros_like(state)
+    loads[5].wait()
     state[:, 0:CHANS] = latent_ref[...]
 
     def sigma(span, extra):
@@ -152,7 +156,7 @@
             shi = sig.astype(BF).astype(F32)
             slo = sig - shi
             line = jnp.where(
-                (lane == CHANS) | (lane == CHANS + 1),
+                (lane == CHANS) | (lane == CHANS + 1) | (lane == CHANS + 4),
                 shi,
                 jnp.where(lane == CHANS + 2, slo, jnp.where(lane == CHANS + 3, 1.0, 0.0)),
             )
@@ -219,9 +223,8 @@
         for h in range(HEADS):
             flat[pl.ds(h, ROWS, stride=HEADS), :] = dot_nt(normed[h], wk[:, h * HD : (h + 1) * HD])
         qk = flat[...]
-        qhi = qk.astype(BF)
-        q2[:, 0:128] = qhi
-        q2[:, 128:256] = (qk - qhi.astype(F32)).astype(BF)
+        rest = pltpu.roll(qk - qk.astype(BF).astype(F32), 4, 1)
+        q2[...] = jnp.where(lane == CHANS + 4, rest, qk).astype(BF)
         acc[...] = jnp.zeros_like(acc)
         top[...] = jnp.full_like(top, -1e30)
         @pl.when(jnp.logical_not(upper) | (s == 1))
@@ -241,7 +244,7 @@
             for e, g in blocks:
                 rows = chunk_of(e, g)[...]
                 plain = rows * pmask.astype(BF) + aug[e][0:1, :].astype(BF)
-                keys.append(jnp.concatenate([plain, plain], axis=1))
+                keys.append(plain)
                 factors.append(dot_nn(rows, spread))
                 turned.append(dot_nt(eye, plain).astype(BF))
             units = [(b, slice(u * COLS, (u + 1) * COLS)) for b in range(len(blocks)) for u in range(QUERIES // COLS)]
@@ -281,20 +284,25 @@
                 gather(*item)
 
         def group(m, carry):
-            key = s * 16 + c * 4 + m
+            @pl.when((s == 0) & (c == 2) & (m == 2))
+            def _():
+                lower_plane(1)
+
+            key = s * 32 + c * 8 + m
             code = jnp.int32(0)
             for ss in range(2):
                 for cc in range(4):
                     for mm, chunks in enumerate(GROUPS[ss][cc]):
-                        here = key == ss * 16 + cc * 4 + mm
+                        here = key == ss * 32 + cc * 8 + mm
                         packed = sum((4 * e + g) << (4 * q) for q, (e, g) in enumerate(chunks))
                         code = jnp.where(here, packed, code)
 
                         @pl.when(here)
                         def _(ss=ss, cc=cc, mm=mm, chunks=chunks):
+                            known = AHEAD.get((ss, cc, mm - 1), [])
                             for e, g in chunks + AHEAD.get((ss, cc, mm), []):
                                 r = e // 2
-                                if e % 2 == cc % 2 and (e, g) not in AHEAD.get((ss, cc, mm - 1), []):
+                                if e % 2 == cc % 2 and (e, g) not in known:
                                     drain(rows_of(0, 0, (4 if g else 3) * PIECE), pr.at[ss, r, g])
                                     if r <= cc // 2 - cc % 2:
                                         ref = grid.at[ss, e, pl.ds(g * CHUNK, CHUNK), :]
@@ -303,23 +311,22 @@
                                 if e % 2 != cc % 2:
                                     drain(rows_of(0, 0, CHUNK), cr.at[ss, e // 2, g])
 
-            @pl.when((s == 0) & (c == 2) & (m == 2))
-            def _():
-                lower_plane(1)
-
             blocks = [((code >> (4 * q + 2)) & 3, (code >> (4 * q)) & 3) for q in range(4)]
 
-            @pl.when(c == 0)
+            short = (c == 0) | ((s == 1) & (((c == 2) & (m > 1)) | ((c == 3) & (m > 2))))
+
+            @pl.when(short)
             def _():
                 attend(blocks[:2])
 
-            @pl.when(c > 0)
+            @pl.when(jnp.logical_not(short))
             def _():
                 attend(blocks)
 
             return carry
 
-        lax.fori_loop(0, jnp.maximum(c + 1, 2), group, 0)
+        groups = jnp.maximum(c + 1, 2) + jnp.where((s == 1) & upper, 1, 0)
+        lax.fori_loop(0, groups, group, 0)
 
         @pl.when((s == 0) & (c == 3))
         def _():
@@ -381,21 +388,23 @@
     both = pl.pallas_call(
         kernel,
         out_shape=jax.ShapeDtypeStruct((2, ROWS, CHANS), F32),
-        in_specs=[smem, smem, vmem, vmem, hbm, hbm, hbm, hbm],
+        in_specs=[smem, smem, hbm, hbm, hbm, hbm, hbm, hbm],
         out_specs=vmem,
         scratch_shapes=[
             pltpu.VMEM((2, 4, SEQ, 128), BF),
+            pltpu.VMEM((ROWS, CHANS), F32),
+            pltpu.VMEM((3, WIDTH), F32),
             pltpu.VMEM((128, WIDTH), BF),
             pltpu.VMEM((128, WIDTH), BF),
             pltpu.VMEM((128, WIDTH), BF),
             pltpu.VMEM((CHANS, WIDTH), BF),
             pltpu.VMEM((4, 8, 128), F32),
             pltpu.VMEM((ROWS, 128), F32),
-            pltpu.VMEM((QUERIES, 256), BF),
+            pltpu.VMEM((QUERIES, 128), BF),
             pltpu.VMEM((QUERIES, 128), F32),
             pltpu.VMEM((128, QUERIES), F32),
             pltpu.VMEM((8, QUERIES), F32),
-            dma((4,)),
+            dma((6,)),
             dma((2,)),
             dma((2, 2)),
             dma((2, 2, 4)),

time: 57.2 us -> 53.7 us (0.939)
  the two profiles are of different devices: /device:TPU:193 before, /device:TPU:225 now
where the time goes in v5:
time: 53.7 us; the launch traced here: 52.6 us
  Pallas kernels  50.6 us (94%)
  local copies, waits for them, and re-layouts  1.35 us (3%)
  between operations  0.64 us (1%)
    pallas_call x1, Pallas kernels, local(): pl.pallas_call(kernel, out_shape=jax.ShapeDtypeStruct((2, ROWS, CHANS), F...  50.6 us
    slice x1, local copies, waits for them, and re-layouts, local(): return (both[0:1], both[1:2])  1.35 us

profile of v5, /device:TPU:225, one launch (start us, length us, event | category | flops | bytes accessed | tf_op | source)
XLA Modules:
  0.0 52.6 jit_solution(14607226919170107738)
XLA Ops:
  0.6 50.6 %shard_map.95 = f32[2,32,64]{2,1,0:T(8,128)} custom-call(s32[4]{0:T(128)} %step_ref.1, f32[2,32]{1,0:T(2,128)} %gain_ref.1, f32[32,64]{1,0:T(8,128)} %bitcast.3, f32[3,4096]{1,0:T(4,128)} %cond_hbm.1, bf16[64,4096]{1,0:T(8,128)(2,1)} %wq_hbm.1, bf16[64,4096]{1,0:T(8,128)(2,1)} %wk_hbm.1, bf16[64,4096]{1,0:T(8,128)(2,1)} %wv_hbm.1, bf16[64,4096]{1,0:T(8,128)(2,1)} %bitcast.2), custom_call_target="tpu_custom_call" | custom-call | tf_op jit(solution)/shard_map/pallas_call | solution.py:388
  51.3 1.3 %fusion = (f32[1,32,64]{2,1,0:T(8,128)}, f32[1,32,64]{2,1,0:T(8,128)}) fusion(f32[2,32,64]{2,1,0:T(8,128)} %shard_map.95), kind=kLoop, calls=%fused_computation | loop fusion | bytes 32768 | tf_op jit(solution)/shard_map/slice | solution.py:419

commit v6 on v5

--- a/solution.py
+++ b/solution.py
@@ -32,15 +32,15 @@
         [
             [(3, 0), (1, 0), (3, 1), (1, 1)],
             [(2, 0), (0, 0), (2, 1), (0, 1)],
-            [(3, 2), (1, 2), (2, 2), (0, 2)],
-            [(3, 3), (1, 3), (2, 3), (0, 3)],
+            [(3, 2), (1, 2), (3, 3), (1, 3)],
+            [(2, 2), (0, 2), (2, 3), (0, 3)],
         ],
     ),
     (
         [[(0, 0), (0, 1)], [(0, 2), (0, 3)]],
         [WHOLE[0], WHOLE[1]],
         [WHOLE[0], WHOLE[1], [(2, 0), (2, 1)], [(2, 2), (2, 3)]],
-        [WHOLE[1], WHOLE[0], [(3, 0), (3, 1), (2, 0), (2, 1)], [(3, 2), (2, 2)], [(3, 3), (2, 3)]],
+        [WHOLE[1], WHOLE[0], [(3, 0), (3, 1), (2, 0), (2, 1)], [(3, 2), (3, 3)], [(2, 2), (2, 3)]],
     ),
 )
 AHEAD = {(1, 2, 1): [(2, 0), (2, 1)], (1, 2, 2): [(2, 2), (2, 3)]}
@@ -181,13 +181,13 @@
             pl.semaphore_wait(barrier, 23)
 
         block = rows_of(c, at, ROWS)
+        @pl.when(jnp.logical_not(upper))
+        def _():
+            for d in range(4):
+                rdma(block, block, zs.at[s], zr.at[s, 0], (across_z, tok(y, d, x))).start()
+
         for d in range(1, 4):
             rdma(block, block, zs.at[s], zr.at[s, zhi], (c, tok(y, (zl + d) & 3, x))).start()
-
-        @pl.when(jnp.logical_not(upper))
-        def _():
-            for d in range(4):
-                rdma(block, block, zs.at[s], zr.at[s, 0], (across_z, tok(y, d, x))).start()
 
         def send_chunk(ss, r, g):
             e = core + 2 * r
@@ -234,8 +234,12 @@
         @pl.when(upper & (s == 0))
         def _():
             drain(rows_of(0, 0, 3 * ROWS), zr.at[s, 1])
+            for g in range(2):
+                send_chunk(s, 1, g)
             drain(rows_of(0, 0, 4 * ROWS), zr.at[s, 0])
-            for g in range(4):
+            for g in range(2):
+                send_chunk(s, 0, g)
+            for g in range(2, 4):
                 for r in range(2):
                     send_chunk(s, r, g)
 

time: 53.7 us -> 53.7 us (level); the launches traced: 52.6 us -> 53.3 us
  Pallas kernels: 50.6 us -> 51.3 us
    pallas_call x1, Pallas kernels: 50.6 us -> 51.3 us  [local(): pl.pallas_call(kernel, out_shape=jax.ShapeDtypeStruct((2, ROWS, CHANS), F...]
where the time goes in v6:
time: 53.7 us; the launch traced here: 53.3 us
  Pallas kernels  51.3 us (96%)
  local copies, waits for them, and re-layouts  1.35 us (3%)
  between operations  0.64 us (1%)
    pallas_call x1, Pallas kernels, local(): pl.pallas_call(kernel, out_shape=jax.ShapeDtypeStruct((2, ROWS, CHANS), F...  51.3 us
    slice x1, local copies, waits for them, and re-layouts, local(): return (both[0:1], both[1:2])  1.35 us

profile of v6, /device:TPU:225, one launch (start us, length us, event | category | flops | bytes accessed | tf_op | source)
XLA Modules:
  0.0 53.3 jit_solution(2834792605307994911)
XLA Ops:
  0.6 51.3 %shard_map.95 = f32[2,32,64]{2,1,0:T(8,128)} custom-call(s32[4]{0:T(128)} %step_ref.1, f32[2,32]{1,0:T(2,128)} %gain_ref.1, f32[32,64]{1,0:T(8,128)} %bitcast.3, f32[3,4096]{1,0:T(4,128)} %cond_hbm.1, bf16[64,4096]{1,0:T(8,128)(2,1)} %wq_hbm.1, bf16[64,4096]{1,0:T(8,128)(2,1)} %wk_hbm.1, bf16[64,4096]{1,0:T(8,128)(2,1)} %wv_hbm.1, bf16[64,4096]{1,0:T(8,128)(2,1)} %bitcast.2), custom_call_target="tpu_custom_call" | custom-call | tf_op jit(solution)/shard_map/pallas_call | solution.py:392
  52.0 1.3 %fusion = (f32[1,32,64]{2,1,0:T(8,128)}, f32[1,32,64]{2,1,0:T(8,128)}) fusion(f32[2,32,64]{2,1,0:T(8,128)} %shard_map.95), kind=kLoop, calls=%fused_computation | loop fusion | bytes 32768 | tf_op jit(solution)/shard_map/slice | solution.py:423

commit v7 on v6

--- a/solution.py
+++ b/solution.py
@@ -40,7 +40,7 @@
         [[(0, 0), (0, 1)], [(0, 2), (0, 3)]],
         [WHOLE[0], WHOLE[1]],
         [WHOLE[0], WHOLE[1], [(2, 0), (2, 1)], [(2, 2), (2, 3)]],
-        [WHOLE[1], WHOLE[0], [(3, 0), (3, 1), (2, 0), (2, 1)], [(3, 2), (3, 3)], [(2, 2), (2, 3)]],
+        [WHOLE[0], WHOLE[1], [(3, 0), (3, 1), (2, 0), (2, 1)], [(3, 2), (3, 3)], [(2, 2), (2, 3)]],
     ),
 )
 AHEAD = {(1, 2, 1): [(2, 0), (2, 1)], (1, 2, 2): [(2, 2), (2, 3)]}

time: 53.7 us -> 53.3 us (level)
  Pallas kernels: 51.3 us -> 50.7 us
    pallas_call x1, Pallas kernels: 51.3 us -> 50.7 us  [local(): pl.pallas_call(kernel, out_shape=jax.ShapeDtypeStruct((2, ROWS, CHANS), F...]
where the time goes in v7:
time: 53.3 us; the launch traced here: 52.7 us
  Pallas kernels  50.7 us (95%)
  local copies, waits for them, and re-layouts  1.35 us (3%)
  between operations  0.64 us (1%)
    pallas_call x1, Pallas kernels, local(): pl.pallas_call(kernel, out_shape=jax.ShapeDtypeStruct((2, ROWS, CHANS), F...  50.7 us
    slice x1, local copies, waits for them, and re-layouts, local(): return (both[0:1], both[1:2])  1.35 us

profile of v7, /device:TPU:225, one launch (start us, length us, event | category | flops | bytes accessed | tf_op | source)
XLA Modules:
  0.0 52.7 jit_solution(6972961603092618429)
XLA Ops:
  0.6 50.7 %shard_map.95 = f32[2,32,64]{2,1,0:T(8,128)} custom-call(s32[4]{0:T(128)} %step_ref.1, f32[2,32]{1,0:T(2,128)} %gain_ref.1, f32[32,64]{1,0:T(8,128)} %bitcast.3, f32[3,4096]{1,0:T(4,128)} %cond_hbm.1, bf16[64,4096]{1,0:T(8,128)(2,1)} %wq_hbm.1, bf16[64,4096]{1,0:T(8,128)(2,1)} %wk_hbm.1, bf16[64,4096]{1,0:T(8,128)(2,1)} %wv_hbm.1, bf16[64,4096]{1,0:T(8,128)(2,1)} %bitcast.2), custom_call_target="tpu_custom_call" | custom-call | tf_op jit(solution)/shard_map/pallas_call | solution.py:392
  51.4 1.3 %fusion = (f32[1,32,64]{2,1,0:T(8,128)}, f32[1,32,64]{2,1,0:T(8,128)}) fusion(f32[2,32,64]{2,1,0:T(8,128)} %shard_map.95), kind=kLoop, calls=%fused_computation | loop fusion | bytes 32768 | tf_op jit(solution)/shard_map/slice | solution.py:423
